TPU v7x, 128 devices: a whole 4x4x4 slice. The times are simulated.
128 devices in a mesh: seq: 8 (over y_hi, x), batch: 16 (over y_lo, z, core).
Axes of the slice: x: 4, y: 4 (y_hi: 2, y_lo: 2; y = y_hi * 2 + y_lo), z: 4, core: 2. Of those that a mesh axis runs over, the one named last changes fastest.
Arguments:
- tokens: bfloat16 [16, 1024, 1536], P('batch', 'seq'), may hold values from -6 to 6
- cotangent: bfloat16 [16, 1024, 1536], P('batch', 'seq'), may hold values from -6 to 6
- segments: int32 [16, 1024], P('batch'), may hold values from 0 to 5, as said below
- routes: int32 [16, 1024, 8], P('batch', 'seq'), may hold values from 0 to 31, all different within a row; in each aligned block of 128 rows (0 to 127, 128 to 255, ..., all dimensions but the last counted through in order) at most 48 rows name the same one
- gate_weights: float32 [16, 1024, 8], P('batch', 'seq'), may hold values from 0.06 to 0.24
- w_query: bfloat16 [1536, 1536], P(('seq', 'batch')), may hold values from -0.15625 to 0.15625
- w_key: bfloat16 [1536, 512], P(('seq', 'batch')), may hold values from -0.15625 to 0.15625
- w_value: bfloat16 [1536, 512], P(('seq', 'batch')), may hold values from -0.15625 to 0.15625
- w_out: bfloat16 [1536, 1536], P(('seq', 'batch')), may hold values from -0.875 to 0.875
- norm_one: bfloat16 [1536], P(('seq', 'batch')), may hold values from 0.5 to 1.5
- norm_two: bfloat16 [1536], P(('seq', 'batch')), may hold values from 0.5 to 1.5
- w_gate: bfloat16 [32, 1536, 512], P('batch', 'seq'), may hold values from -0.15625 to 0.15625
- w_up: bfloat16 [32, 1536, 512], P('batch', 'seq'), may hold values from -0.15625 to 0.15625
- w_down: bfloat16 [32, 512, 1536], P('batch', 'seq'), may hold values from -1 to 1
Outputs:
- output: bfloat16 [16, 1024, 1536], P('batch', 'seq')
- grad_tokens: bfloat16 [16, 1024, 1536], P('batch', 'seq')
- grad_w_query: float32 [1536, 1536], P(('seq', 'batch'))
- grad_w_key: float32 [1536, 512], P(('seq', 'batch'))
- grad_w_value: float32 [1536, 512], P(('seq', 'batch'))
- grad_w_out: float32 [1536, 1536], P(('seq', 'batch'))
- grad_norm_one: float32 [1536], P(('seq', 'batch'))
- grad_norm_two: float32 [1536], P(('seq', 'batch'))
- grad_w_gate: float32 [32, 1536, 512], P('batch', 'seq')
- grad_w_up: float32 [32, 1536, 512], P('batch', 'seq')
- grad_w_down: float32 [32, 512, 1536], P('batch', 'seq')
Inputs may be any that keep to these rules, and one draw needn't show every extreme that they name: `segments`: along each sequence the segment numbers start at 0 and never fall, rising by one at each document boundary; whole documents hold 204 to 801 tokens, or in one of the sequences up to 1023; the first and last document of a sequence may be cut by its ends. `routes`: each token names 8 different experts; among the 128 tokens of one device (aligned blocks of rows) no expert is named more than 48 times, a bound that some block reaches.
All inputs are finite; a program needn't handle non-finite values.
Results may differ from a plain program's by a relative error of at most 0.019.
Values may be sent and summed in bfloat16 or wider, within the bound.
No kernel may reach another device: no remote copies, remote signals or barrier semaphores. Data moves between devices by JAX's collectives and lax.ppermute only.
A program may use at most 192 MiB of HBM per device.

v0:
```python
import jax
import jax.numpy as jnp
from jax import lax
from jax.sharding import PartitionSpec as P

HEAD_DIM = 64
TOPK = 8


norm_eps = 1e-06
rope_base = 10000.0
masked_score = -1e30


def rms_scale(values):
    return lax.rsqrt(jnp.mean(values * values, axis=-1, keepdims=True) + norm_eps)


def rotate(values, cosine, sine):
    half_dim = values.shape[-1] // 2
    turned = jnp.concatenate([-values[..., half_dim:], values[..., :half_dim]], axis=-1)
    return values * cosine + turned * sine


def rope_tables(position):
    freq_index = jnp.arange(HEAD_DIM // 2, dtype=jnp.float32) * (2.0 / HEAD_DIM)
    frequency = rope_base ** (-freq_index)
    angle = position.astype(jnp.float32)[..., None] * frequency
    angle = jnp.concatenate([angle, angle], axis=-1)
    return (jnp.cos(angle), jnp.sin(angle))


def mask_scores(query_heads, key_heads, allowed, score_scale):
    scores = (
        jnp.einsum("qkgd,tkd->kgqt", query_heads, key_heads, preferred_element_type=jnp.float32)
        * score_scale
    )
    return jnp.where(allowed[None, None], scores, masked_score)


def shards(
    tokens,
    cotangent,
    segments,
    routes,
    gate_weights,
    w_query,
    w_key,
    w_value,
    w_out,
    norm_one,
    norm_two,
    w_gate,
    w_up,
    w_down,
):
    row_count = tokens.shape[1]
    features = tokens.shape[2]
    seq_length = segments.shape[1]
    query_width = w_query.shape[1]
    kv_width = w_key.shape[1]
    head_count = query_width // HEAD_DIM
    kv_count = kv_width // HEAD_DIM
    group_size = head_count // kv_count
    score_scale = HEAD_DIM ** (-0.5)
    local_experts = w_gate.shape[0]
    expert_count = local_experts * lax.axis_size("batch")
    capacity = row_count * TOPK * 3 // (2 * expert_count)
    pair_count = row_count * TOPK
    buffer_shape = (expert_count * capacity, features)
    full_query, full_key, full_value, full_out, gain_one, gain_two = (
        lax.all_gather(w_query, ("seq", "batch"), axis=0, tiled=True),
        lax.all_gather(w_key, ("seq", "batch"), axis=0, tiled=True),
        lax.all_gather(w_value, ("seq", "batch"), axis=0, tiled=True),
        lax.all_gather(w_out, ("seq", "batch"), axis=0, tiled=True),
        lax.all_gather(norm_one, ("seq", "batch"), axis=0, tiled=True),
        lax.all_gather(norm_two, ("seq", "batch"), axis=0, tiled=True),
    )
    gate_full, up_full, down_full = (
        lax.all_gather(w_gate, "seq", axis=1, tiled=True),
        lax.all_gather(w_up, "seq", axis=1, tiled=True),
        lax.all_gather(w_down, "seq", axis=1, tiled=True),
    )
    inputs = tokens[0].astype(jnp.float32)
    upstream = cotangent[0].astype(jnp.float32)
    scale_one = rms_scale(inputs)
    normed_one = (inputs * scale_one * gain_one.astype(jnp.float32)).astype(jnp.bfloat16)
    seg_all = segments[0]
    own_start = lax.axis_index("seq") * row_count
    own_seg = lax.dynamic_slice_in_dim(seg_all, own_start, row_count)
    own_place = own_start + jnp.arange(row_count, dtype=jnp.int32)
    earlier = jnp.sum((seg_all[None, :] < own_seg[:, None]).astype(jnp.int32), axis=1)
    cosine, sine = rope_tables(own_place - earlier)
    cosine = cosine[:, None, :]
    sine = sine[:, None, :]
    query_raw = jnp.dot(normed_one, full_query, preferred_element_type=jnp.float32)
    key_raw = jnp.dot(normed_one, full_key, preferred_element_type=jnp.float32)
    value_raw = jnp.dot(normed_one, full_value, preferred_element_type=jnp.float32)
    queries = rotate(query_raw.reshape(row_count, head_count, HEAD_DIM), cosine, sine).astype(
        jnp.bfloat16
    )
    query_heads = queries.reshape(row_count, kv_count, group_size, HEAD_DIM)
    key_own = (
        rotate(key_raw.reshape(row_count, kv_count, HEAD_DIM), cosine, sine)
        .astype(jnp.bfloat16)
        .reshape(row_count, kv_width)
    )
    value_own = value_raw.astype(jnp.bfloat16)
    key_all, value_all = (
        lax.all_gather(key_own, "seq", axis=0, tiled=True),
        lax.all_gather(value_own, "seq", axis=0, tiled=True),
    )
    key_heads = key_all.reshape(seq_length, kv_count, HEAD_DIM)
    value_heads = value_all.reshape(seq_length, kv_count, HEAD_DIM)
    key_place = jnp.arange(seq_length, dtype=jnp.int32)
    allowed = (seg_all[None, :] == own_seg[:, None]) & (key_place[None, :] <= own_place[:, None])
    scores = mask_scores(query_heads, key_heads, allowed, score_scale)
    row_max = jnp.max(scores, axis=-1, keepdims=True)
    exp_scores = jnp.exp(scores - row_max)
    denominator = jnp.sum(exp_scores, axis=-1, keepdims=True)
    soft_low = (exp_scores / denominator).astype(jnp.bfloat16)
    log_total = row_max + jnp.log(denominator)
    mixed = jnp.einsum("kgqt,tkd->qkgd", soft_low, value_heads, preferred_element_type=jnp.float32)
    mixed = mixed.reshape(row_count, query_width).astype(jnp.bfloat16)
    hidden = inputs + jnp.dot(mixed, full_out, preferred_element_type=jnp.float32)
    scale_two = rms_scale(hidden)
    normed_two = (hidden * scale_two * gain_two.astype(jnp.float32)).astype(jnp.bfloat16)
    flat_route = routes[0].reshape(pair_count)
    hits = (flat_route[:, None] == jnp.arange(expert_count, dtype=jnp.int32)[None, :]).astype(
        jnp.int32
    )
    slot_index = jnp.sum((jnp.cumsum(hits, axis=0) - 1) * hits, axis=1)
    destination = flat_route * capacity + slot_index
    token_of = jnp.arange(pair_count, dtype=jnp.int32) // TOPK
    send_rows = jnp.zeros(buffer_shape, jnp.bfloat16).at[destination].set(normed_two[token_of])
    expert_in = lax.all_to_all(send_rows, "batch", split_axis=0, concat_axis=0, tiled=True)
    expert_in = expert_in.reshape(-1, local_experts, capacity, features)
    gate_pre = jnp.einsum(
        "secd,edf->secf", expert_in, gate_full, preferred_element_type=jnp.float32
    )
    up_pre = jnp.einsum("secd,edf->secf", expert_in, up_full, preferred_element_type=jnp.float32)
    activated = (jax.nn.silu(gate_pre) * up_pre).astype(jnp.bfloat16)
    expert_out = jnp.einsum(
        "secf,efd->secd", activated, down_full, preferred_element_type=jnp.float32
    ).astype(jnp.bfloat16)
    returned = lax.all_to_all(
        expert_out.reshape(buffer_shape), "batch", split_axis=0, concat_axis=0, tiled=True
    )
    pair_gate = gate_weights[0]
    pair_out = returned[destination].astype(jnp.float32).reshape(row_count, TOPK, features)
    output = hidden + jnp.sum(pair_gate[:, :, None] * pair_out, axis=1)
    gate_back, up_back, down_back = (
        lax.all_gather(w_gate, "seq", axis=1, tiled=True),
        lax.all_gather(w_up, "seq", axis=1, tiled=True),
        lax.all_gather(w_down, "seq", axis=1, tiled=True),
    )
    grad_pair = (
        (pair_gate[:, :, None] * upstream[:, None, :])
        .reshape(pair_count, features)
        .astype(jnp.bfloat16)
    )
    send_grad = jnp.zeros(buffer_shape, jnp.bfloat16).at[destination].set(grad_pair)
    grad_in = lax.all_to_all(send_grad, "batch", split_axis=0, concat_axis=0, tiled=True)
    grad_in = grad_in.reshape(-1, local_experts, capacity, features)
    grad_act = jnp.einsum("secd,efd->secf", grad_in, down_back, preferred_element_type=jnp.float32)
    grad_down = jnp.einsum("secf,secd->efd", activated, grad_in, preferred_element_type=jnp.float32)
    sigmoid_gate = jax.nn.sigmoid(gate_pre)
    grad_gate_pre = (
        grad_act * up_pre * sigmoid_gate * (1.0 + gate_pre * (1.0 - sigmoid_gate))
    ).astype(jnp.bfloat16)
    grad_up_pre = (grad_act * gate_pre * sigmoid_gate).astype(jnp.bfloat16)
    grad_gate_w = jnp.einsum(
        "secd,secf->edf", expert_in, grad_gate_pre, preferred_element_type=jnp.float32
    )
    grad_up_w = jnp.einsum(
        "secd,secf->edf", expert_in, grad_up_pre, preferred_element_type=jnp.float32
    )
    grad_rows = jnp.einsum(
        "secf,edf->secd", grad_gate_pre, gate_back, preferred_element_type=jnp.float32
    )
    grad_rows = grad_rows + jnp.einsum(
        "secf,edf->secd", grad_up_pre, up_back, preferred_element_type=jnp.float32
    )
    grad_back = lax.all_to_all(
        grad_rows.astype(jnp.bfloat16).reshape(buffer_shape),
        "batch",
        split_axis=0,
        concat_axis=0,
        tiled=True,
    )
    grad_normed_two = jnp.sum(
        grad_back[destination].astype(jnp.float32).reshape(row_count, TOPK, features), axis=1
    )
    query_back, key_back, value_back, out_back, gain_one_back, gain_two_back = (
        lax.all_gather(w_query, ("seq", "batch"), axis=0, tiled=True),
        lax.all_gather(w_key, ("seq", "batch"), axis=0, tiled=True),
        lax.all_gather(w_value, ("seq", "batch"), axis=0, tiled=True),
        lax.all_gather(w_out, ("seq", "batch"), axis=0, tiled=True),
        lax.all_gather(norm_one, ("seq", "batch"), axis=0, tiled=True),
        lax.all_gather(norm_two, ("seq", "batch"), axis=0, tiled=True),
    )
    scaled_two = gain_two_back.astype(jnp.float32) * grad_normed_two
    grad_gain_two = jnp.sum(grad_normed_two * hidden * scale_two, axis=0)
    grad_hidden = (
        upstream
        + scale_two * scaled_two
        - hidden * scale_two**3 * jnp.mean(scaled_two * hidden, axis=-1, keepdims=True)
    )
    grad_z = grad_hidden.astype(jnp.bfloat16)
    grad_out_w = jnp.dot(mixed.T, grad_z, preferred_element_type=jnp.float32)
    grad_mixed = jnp.dot(grad_z, out_back.T, preferred_element_type=jnp.float32).astype(
        jnp.bfloat16
    )
    grad_mixed_heads = grad_mixed.reshape(row_count, kv_count, group_size, HEAD_DIM)
    again_scores = mask_scores(query_heads, key_heads, allowed, score_scale)
    soft_again = jnp.exp(again_scores - log_total)
    soft_again_low = soft_again.astype(jnp.bfloat16)
    grad_soft = jnp.einsum(
        "qkgd,tkd->kgqt", grad_mixed_heads, value_heads, preferred_element_type=jnp.float32
    )
    row_dot = jnp.sum(soft_again * grad_soft, axis=-1, keepdims=True)
    grad_scores = (soft_again * (grad_soft - row_dot)).astype(jnp.bfloat16)
    grad_query_rot = (
        jnp.einsum("kgqt,tkd->qkgd", grad_scores, key_heads, preferred_element_type=jnp.float32)
        * score_scale
    )
    grad_key_part = (
        jnp.einsum("kgqt,qkgd->tkd", grad_scores, query_heads, preferred_element_type=jnp.float32)
        * score_scale
    )
    grad_value_part = jnp.einsum(
        "kgqt,qkgd->tkd", soft_again_low, grad_mixed_heads, preferred_element_type=jnp.float32
    )
    grad_key_own, grad_value_own = (
        lax.psum_scatter(
            grad_key_part.reshape(seq_length, kv_width).astype(jnp.bfloat16),
            "seq",
            scatter_dimension=0,
            tiled=True,
        ).astype(jnp.float32),
        lax.psum_scatter(
            grad_value_part.reshape(seq_length, kv_width).astype(jnp.bfloat16),
            "seq",
            scatter_dimension=0,
            tiled=True,
        ).astype(jnp.float32),
    )
    grad_query_low = rotate(grad_query_rot.reshape(row_count, head_count, HEAD_DIM), cosine, -sine)
    grad_query_low = grad_query_low.reshape(row_count, query_width).astype(jnp.bfloat16)
    grad_key_low = rotate(grad_key_own.reshape(row_count, kv_count, HEAD_DIM), cosine, -sine)
    grad_key_low = grad_key_low.reshape(row_count, kv_width).astype(jnp.bfloat16)
    grad_value_low = grad_value_own.astype(jnp.bfloat16)
    grad_query_w = jnp.dot(normed_one.T, grad_query_low, preferred_element_type=jnp.float32)
    grad_key_w = jnp.dot(normed_one.T, grad_key_low, preferred_element_type=jnp.float32)
    grad_value_w = jnp.dot(normed_one.T, grad_value_low, preferred_element_type=jnp.float32)
    grad_normed_one = jnp.dot(grad_query_low, query_back.T, preferred_element_type=jnp.float32)
    grad_normed_one = grad_normed_one + jnp.dot(
        grad_key_low, key_back.T, preferred_element_type=jnp.float32
    )
    grad_normed_one = grad_normed_one + jnp.dot(
        grad_value_low, value_back.T, preferred_element_type=jnp.float32
    )
    scaled_one = gain_one_back.astype(jnp.float32) * grad_normed_one
    grad_gain_one = jnp.sum(grad_normed_one * inputs * scale_one, axis=0)
    grad_inputs = (
        grad_hidden
        + scale_one * scaled_one
        - inputs * scale_one**3 * jnp.mean(scaled_one * inputs, axis=-1, keepdims=True)
    )
    sum_query, sum_key, sum_value, sum_out, sum_gain_one, sum_gain_two = (
        lax.psum_scatter(grad_query_w, ("seq", "batch"), scatter_dimension=0, tiled=True),
        lax.psum_scatter(grad_key_w, ("seq", "batch"), scatter_dimension=0, tiled=True),
        lax.psum_scatter(grad_value_w, ("seq", "batch"), scatter_dimension=0, tiled=True),
        lax.psum_scatter(grad_out_w, ("seq", "batch"), scatter_dimension=0, tiled=True),
        lax.psum_scatter(grad_gain_one, ("seq", "batch"), scatter_dimension=0, tiled=True),
        lax.psum_scatter(grad_gain_two, ("seq", "batch"), scatter_dimension=0, tiled=True),
    )
    sum_gate, sum_up, sum_down = (
        lax.psum_scatter(
            grad_gate_w.astype(jnp.bfloat16), "seq", scatter_dimension=1, tiled=True
        ).astype(jnp.float32),
        lax.psum_scatter(
            grad_up_w.astype(jnp.bfloat16), "seq", scatter_dimension=1, tiled=True
        ).astype(jnp.float32),
        lax.psum_scatter(
            grad_down.astype(jnp.bfloat16), "seq", scatter_dimension=1, tiled=True
        ).astype(jnp.float32),
    )
    return (
        output.astype(jnp.bfloat16)[None],
        grad_inputs.astype(jnp.bfloat16)[None],
        sum_query,
        sum_key,
        sum_value,
        sum_out,
        sum_gain_one,
        sum_gain_two,
        sum_gate,
        sum_up,
        sum_down,
    )


def solution(mesh):
    placed = (
        P("batch", "seq", None),
        P("batch", "seq", None),
        P("batch", None),
        P("batch", "seq", None),
        P("batch", "seq", None),
        P(("seq", "batch"), None),
        P(("seq", "batch"), None),
        P(("seq", "batch"), None),
        P(("seq", "batch"), None),
        P(("seq", "batch")),
        P(("seq", "batch")),
        P("batch", "seq", None),
        P("batch", "seq", None),
        P("batch", "seq", None),
    )
    return jax.shard_map(
        shards,
        mesh=mesh,
        in_specs=placed,
        out_specs=(
            P("batch", "seq", None),
            P("batch", "seq", None),
            P(("seq", "batch"), None),
            P(("seq", "batch"), None),
            P(("seq", "batch"), None),
            P(("seq", "batch"), None),
            P(("seq", "batch")),
            P(("seq", "batch")),
            P("batch", "seq", None),
            P("batch", "seq", None),
            P("batch", "seq", None),
        ),
        check_vma=False,
    )
```

profile of v0, /device:TPU:8, one launch (start us, length us, event | category | flops | bytes accessed | tf_op | source)
XLA Modules:
  0.0 2443.8 jit_solution(2467610615860445771)
XLA Ops:
  10.4 66.9 %all-reduce.13 = (bf16[1536]{0:T(1024)(128)(2,1)S(1)}, bf16[1536]{0:T(1024)(128)(2,1)S(1)}) all-reduce(bf16[1536]{0:T(1024)(128)(2,1)S(1)} %dynamic-update-slice, bf16[1536]{0:T(1024)(128)(2,1)S(1)} %dynamic-update-slice.1), channel_id=1, replica_groups=mesh['seq'=8,'batch'=16] {'seq','batch'}, use_global_device_ids=true, to_apply=%add | all-reduce | flops 3072 | bytes 12288
  79.0 126.9 %all-gather.24.cloned.1.call-done = bf16[128,12,512]{2,1,0:T(8,128)(2,1)} async-done(((bf16[1,12,512]{2,1,0:T(8,128)(2,1)}), bf16[128,12,512]{2,1,0:T(8,128)(2,1)}) %all-gather.24.cloned.1.call-update) | async-done | bytes 1572880 | tf_op jit(solution)/shard_map/all_gather | solution.py:74
  212.6 187.9 %all-gather.26.cloned.1.call-done = bf16[128,12,512]{2,1,0:T(8,128)(2,1)} async-done(((bf16[1,12,512]{2,1,0:T(8,128)(2,1)}), bf16[128,12,512]{2,1,0:T(8,128)(2,1)}) %all-gather.26.cloned.1.call-update) | async-done | bytes 1572880 | tf_op jit(solution)/shard_map/all_gather | solution.py:73
  421.6 27.2 %all-gather.14.cloned.1.call-done = bf16[1024,512]{1,0:T(8,128)(2,1)} async-done(((bf16[128,512]{1,0:T(8,128)(2,1)}), bf16[1024,512]{1,0:T(8,128)(2,1)}) %all-gather.14.cloned.1.call-update) | async-done | bytes 1048592 | tf_op jit(solution)/shard_map/all_gather | solution.py:111
  450.3 200.7 %all-gather.28.cloned.1.call-done = bf16[128,12,1536]{2,1,0:T(8,128)(2,1)} async-done(((bf16[1,12,1536]{2,1,0:T(8,128)(2,1)}), bf16[128,12,1536]{2,1,0:T(8,128)(2,1)}) %all-gather.28.cloned.1.call-update) | async-done | bytes 4718608 | tf_op jit(solution)/shard_map/all_gather | solution.py:72
  670.0 29.8 %all-gather.16.cloned.1.call-done = bf16[1024,512]{0,1:T(8,128)(2,1)} async-done(((bf16[128,512]{0,1:T(8,128)(2,1)}), bf16[1024,512]{0,1:T(8,128)(2,1)}) %all-gather.16.cloned.1.call-update) | async-done | bytes 1048592 | tf_op jit(solution)/shard_map/all_gather | solution.py:110
  710.1 192.0 %all-gather.30.cloned.1.call-done = bf16[128,12,1536]{2,1,0:T(8,128)(2,1)} async-done(((bf16[1,12,1536]{2,1,0:T(8,128)(2,1)}), bf16[128,12,1536]{2,1,0:T(8,128)(2,1)}) %all-gather.30.cloned.1.call-update) | async-done | bytes 4718608 | tf_op jit(solution)/shard_map/all_gather | solution.py:75
  918.4 19.6 scatter_custom_fusion
  953.6 59.8 %all-to-all-done = bf16[16,96,1536]{2,1,0:T(8,128)(2,1)} async-done(((bf16[16,96,1536]{2,1,0:T(8,128)(2,1)}), bf16[16,96,1536]{2,1,0:T(8,128)(2,1)}, u32[]{:S(2)}, u32[]{:S(2)}) %all-to-all-start) | async-done | bytes 4718624 | tf_op jit(solution)/shard_map/all_to_all | solution.py:136
  1013.4 17.9 all-to-all-start.2
  1050.4 46.9 %all-to-all-done.2 = bf16[16,96,1536]{2,1,0:T(8,128)(2,1)} async-done(((bf16[16,96,1536]{2,1,0:T(8,128)(2,1)}), bf16[16,96,1536]{2,1,0:T(8,128)(2,1)}, u32[]{:S(2)}, u32[]{:S(2)}) %all-to-all-start.2) | async-done | bytes 4718624 | tf_op jit(solution)/shard_map/all_to_all | solution.py:163
  1097.3 26.1 %all-gather.22.cloned.1.call-done = bf16[2,512,1536]{2,1,0:T(8,128)(2,1)} async-done(((bf16[2,64,1536]{2,1,0:T(8,128)(2,1)}), bf16[2,512,1536]{2,1,0:T(8,128)(2,1)}) %all-gather.22.cloned.1.call-update) | async-done | bytes 3145744 | tf_op jit(solution)/shard_map/all_gather | solution.py:82
  1159.9 50.5 %all-to-all-done.1 = bf16[16,96,1536]{2,1,0:T(8,128)(2,1)} async-done(((bf16[16,96,1536]{2,1,0:T(8,128)(2,1)}), bf16[16,96,1536]{2,1,0:T(8,128)(2,1)}, u32[]{:S(2)}, u32[]{:S(2)}) %all-to-all-start.1) | async-done | bytes 4718624 | tf_op jit(solution)/shard_map/all_to_all | solution.py:146
  1210.4 12.6 all-to-all-start.3
  1233.8 51.5 %all-to-all-done.3 = bf16[16,96,1536]{2,1,0:T(8,128)(2,1)} async-done(((bf16[16,96,1536]{2,1,0:T(8,128)(2,1)}), bf16[16,96,1536]{2,1,0:T(8,128)(2,1)}, u32[]{:S(2)}, u32[]{:S(2)}) %all-to-all-start.3) | async-done | bytes 4718624 | tf_op jit(solution)/shard_map/all_to_all | solution.py:184
  1380.3 32.3 %reduce-scatter.24.cloned.1.call-done = bf16[128,512]{1,0:T(8,128)(2,1)} async-done(((bf16[1024,512]{1,0:T(8,128)(2,1)}), bf16[128,512]{1,0:T(8,128)(2,1)}) %reduce-scatter.24.cloned.1.call-update) | async-done | bytes 131088
  1416.2 71.6 %reduce-scatter.26.cloned.1.call-done = bf16[128,512]{1,0:T(8,128)(2,1)} async-done(((bf16[1024,512]{1,0:T(8,128)(2,1)}), bf16[128,512]{1,0:T(8,128)(2,1)}) %reduce-scatter.26.cloned.1.call-update) | async-done | bytes 131088
  1491.0 363.4 %fusion.107 = (f32[16,1536]{1,0:T(8,128)S(1)}, f32[16,512]{1,0:T(8,128)S(1)}, f32[16,512]{1,0:T(8,128)S(1)}, f32[16,1536]{1,0:T(8,128)S(1)}) fusion(f32[1536,1536]{1,0:T(8,128)} %fusion.81, f32[1536,512]{1,0:T(8,128)} %fusion.104, f32[1536,512]{1,0:T(8,128)} %fusion.102, f32[1536,1536]{1,0:T(8,128)} %fusion.86), kind=kCustom, calls=%all-reduce-scatter.4 | all-reduce-scatter fusion | flops 8388609 | bytes 25427968
  1861.0 39.7 %collective-permute-start.59 = (f32[16,512]{1,0:T(8,128)S(1)}, f32[16,512]{1,0:T(8,128)S(1)}, u32[]{:S(2)}, u32[]{:S(2)}) collective-permute-start(f32[16,512]{1,0:T(8,128)S(1)} %get-tuple-element.24), channel_id=1, source_target_pairs={{0,28},{1,29},{2,30},{3,31},{4,32},{5,33},{6,34},{7,35},{8,36},{9,... | collective-permute-start | bytes 98312
  2195.7 65.2 %all-reduce.12 = (f32[1536]{0:T(1024)S(1)}, f32[1536]{0:T(1024)S(1)}) all-reduce(f32[1536]{0:T(1024)S(1)} %get-tuple-element.13, f32[1536]{0:T(1024)S(1)} %get-tuple-element.11), channel_id=8, replica_groups=mesh['seq'=8,'batch'=16] {'seq','batch'}, use_global_device_ids=true, to_apply=%region_22.23.clone | all-reduce | flops 3072 | bytes 24576
  2262.1 26.6 %concatenate.35 = f32[524,512]{1,0:T(8,128)S(1)} concatenate(f32[12,512]{1,0:T(8,128)} %copy-done.78, f32[16,512]{1,0:T(8,128)} %copy-done.76, f32[16,512]{1,0:T(8,128)} %copy-done.77, f32[16,512]{1,0:T(8,128)} %copy-done.79, f32[16,512]{1,0:T(8,128)} %copy-done.80, f32[16,512]{1,0:T(8,128)} %copy-done.81, f32[16,512]{1,0:T(8,128)} %copy-done.82, f32[16,512]{1,0:T(8,128)} %copy-done.83, ...), dimensions={0} | concatenate | bytes 2146304
  2288.7 26.6 %concatenate.36 = f32[524,512]{1,0:T(8,128)S(1)} concatenate(f32[12,512]{1,0:T(8,128)} %copy-done.75, f32[16,512]{1,0:T(8,128)} %copy-done.108, f32[16,512]{1,0:T(8,128)} %copy-done.109, f32[16,512]{1,0:T(8,128)} %copy-done.110, f32[16,512]{1,0:T(8,128)} %copy-done.111, f32[16,512]{1,0:T(8,128)} %copy-done.112, f32[16,512]{1,0:T(8,128)} %collective-permute-done.89, ...), dimensions={0} | concatenate | bytes 2146304
  2351.7 31.7 %concatenate.34 = f32[524,1536]{1,0:T(8,128)S(1)} concatenate(f32[12,1536]{1,0:T(8,128)} %copy-done.35, f32[16,1536]{1,0:T(8,128)} %copy-done.33, f32[16,1536]{1,0:T(8,128)} %copy-done.34, f32[16,1536]{1,0:T(8,128)} %copy-done.36, f32[16,1536]{1,0:T(8,128)} %copy-done.37, f32[16,1536]{1,0:T(8,128)} %copy-done.38, f32[16,1536]{1,0:T(8,128)} %copy-done.39, f32[16,1536]{1,0:T(8,128)} %copy-done.40, ...), dimensions={0} | concatenate | bytes 6438912
  2405.5 30.9 %concatenate.37 = f32[524,1536]{1,0:T(8,128)S(1)} concatenate(f32[12,1536]{1,0:T(8,128)} %copy-done.32, f32[16,1536]{1,0:T(8,128)} %copy-done.51, f32[16,1536]{1,0:T(8,128)} %copy-done.52, f32[16,1536]{1,0:T(8,128)} %copy-done.53, f32[16,1536]{1,0:T(8,128)} %copy-done.54, f32[16,1536]{1,0:T(8,128)} %copy-done.55, f32[16,1536]{1,0:T(8,128)} %copy-done.56, f32[16,1536]{1,0:T(8,128)} %copy-done.59, ...), dimensions={0} | concatenate | bytes 6438912
  (671 shorter events, 621.7 us)
Async XLA Ops:
  7.2 198.8 %all-gather.24.cloned.1.call-start = ((), (), s32[]{:S(2)}) async-start(), calls=%async_computation.17 | async-start | bytes 2113536 | tf_op jit(solution)/shard_map/all_gather | solution.py:74
  7.9 392.6 %all-gather.26.cloned.1.call-start = ((), (), s32[]{:S(2)}) async-start(), calls=%async_computation.18 | async-start | bytes 2113536 | tf_op jit(solution)/shard_map/all_gather | solution.py:73
  8.7 440.2 %all-gather.14.cloned.1.call-start = ((), (), s32[]{:S(2)}) async-start(), calls=%async_computation.9 | async-start | bytes 1179648 | tf_op jit(solution)/shard_map/all_gather | solution.py:111
  210.9 440.1 %all-gather.28.cloned.1.call-start = ((), (), s32[]{:S(2)}) async-start(), calls=%async_computation.19 | async-start | bytes 6340608 | tf_op jit(solution)/shard_map/all_gather | solution.py:72
  211.5 488.4 %all-gather.16.cloned.1.call-start = ((), (), s32[]{:S(2)}) async-start(), calls=%async_computation.10 | async-start | bytes 1179648 | tf_op jit(solution)/shard_map/all_gather | solution.py:110
  407.5 494.6 %all-gather.30.cloned.1.call-start = ((), (), s32[]{:S(2)}) async-start(), calls=%async_computation.20 | async-start | bytes 6340608 | tf_op jit(solution)/shard_map/all_gather | solution.py:75
  408.1 623.3 %all-gather.20.cloned.1.call-start = ((), (), s32[]{:S(2)}) async-start(), calls=%async_computation.12 | async-start | bytes 3538944 | tf_op jit(solution)/shard_map/all_gather | solution.py:81
  408.8 634.0 %all-gather.18.cloned.1.call-start = ((), (), s32[]{:S(2)}) async-start(), calls=%async_computation.11 | async-start | bytes 3538944 | tf_op jit(solution)/shard_map/all_gather | solution.py:80
  938.0 75.4 %all-to-all-start = ((bf16[16,96,1536]{2,1,0:T(8,128)(2,1)}), bf16[16,96,1536]{2,1,0:T(8,128)(2,1)}, u32[]{:S(2)}, u32[]{:S(2)}) async-start(bf16[16,96,1536]{2,1,0:T(8,128)(2,1)} %bitcast.303), calls=%async_computation | async-start | bytes 9437184 | tf_op jit(solution)/shard_map/all_to_all | solution.py:136
  943.6 179.8 %all-gather.22.cloned.1.call-start = ((), (), s32[]{:S(2)}) async-start(), calls=%async_computation.13 | async-start | bytes 3538944 | tf_op jit(solution)/shard_map/all_gather | solution.py:82
  1013.4 83.9 %all-to-all-start.2 = ((bf16[16,96,1536]{2,1,0:T(8,128)(2,1)}), bf16[16,96,1536]{2,1,0:T(8,128)(2,1)}, u32[]{:S(2)}, u32[]{:S(2)}) async-start(bf16[16,96,1536]{2,1,0:T(8,128)(2,1)} %bitcast.304), calls=%async_computation.2 | async-start | bytes 9437184 | tf_op jit(solution)/shard_map/all_to_all | solution.py:163
  1139.5 70.9 %all-to-all-start.1 = ((bf16[16,96,1536]{2,1,0:T(8,128)(2,1)}), bf16[16,96,1536]{2,1,0:T(8,128)(2,1)}, u32[]{:S(2)}, u32[]{:S(2)}) async-start(bf16[16,96,1536]{2,1,0:T(8,128)(2,1)} %bitcast.306), calls=%async_computation.1 | async-start | bytes 9437184 | tf_op jit(solution)/shard_map/all_to_all | solution.py:146
  1210.4 74.9 %all-to-all-start.3 = ((bf16[16,96,1536]{2,1,0:T(8,128)(2,1)}), bf16[16,96,1536]{2,1,0:T(8,128)(2,1)}, u32[]{:S(2)}, u32[]{:S(2)}) async-start(bf16[16,96,1536]{2,1,0:T(8,128)(2,1)} %bitcast.305), calls=%async_computation.3 | async-start | bytes 9437184 | tf_op jit(solution)/shard_map/all_to_all | solution.py:184
  1223.0 189.6 %reduce-scatter.24.cloned.1.call-start = ((), (), s32[]{:S(2)}) async-start(), calls=%async_computation.21 | async-start | bytes 1179648
  1335.2 152.6 %reduce-scatter.26.cloned.1.call-start = ((), (), s32[]{:S(2)}) async-start(), calls=%async_computation.22 | async-start | bytes 1179648
  1344.2 790.7 %reduce-scatter.22.cloned.1.call-start = ((), (), s32[]{:S(2)}) async-start(), calls=%async_computation.16 | async-start | bytes 3538944 | tf_op jit(solution)/shard_map/reduce_scatter | solution.py:285
  1351.5 785.4 %reduce-scatter.20.cloned.1.call-start = ((), (), s32[]{:S(2)}) async-start(), calls=%async_computation.15 | async-start | bytes 3538944 | tf_op jit(solution)/shard_map/reduce_scatter | solution.py:282
  1358.8 780.1 %reduce-scatter.18.cloned.1.call-start = ((), (), s32[]{:S(2)}) async-start(), calls=%async_computation.14 | async-start | bytes 3538944 | tf_op jit(solution)/shard_map/reduce_scatter | solution.py:279
  2184.3 131.1 %collective-permute-start.115 = (f32[16,1536]{1,0:T(8,128)S(1)}, f32[16,1536]{1,0:T(8,128)}, u32[]{:S(2)}, u32[]{:S(2)}) collective-permute-start(f32[16,1536]{1,0:T(8,128)S(1)} %get-tuple-element.26), channel_id=1, source_target_pairs={{0,20},{1,21},{2,22},{3,23},{4,24},{5,25},{6,26},{7,27},{8,28},{9,... | collective-permute-start | bytes 294920
  2186.2 132.0 %collective-permute-start.114 = (f32[16,1536]{1,0:T(8,128)S(1)}, f32[16,1536]{1,0:T(8,128)}, u32[]{:S(2)}, u32[]{:S(2)}) collective-permute-start(f32[16,1536]{1,0:T(8,128)S(1)} %get-tuple-element.26), channel_id=1, source_target_pairs={{0,19},{1,20},{2,21},{3,22},{4,23},{5,24},{6,25},{7,26},{8,27},{9,... | collective-permute-start | bytes 294920
  2188.1 132.9 %collective-permute-start.113 = (f32[16,1536]{1,0:T(8,128)S(1)}, f32[16,1536]{1,0:T(8,128)}, u32[]{:S(2)}, u32[]{:S(2)}) collective-permute-start(f32[16,1536]{1,0:T(8,128)S(1)} %get-tuple-element.26), channel_id=1, source_target_pairs={{0,18},{1,19},{2,20},{3,21},{4,22},{5,23},{6,24},{7,25},{8,26},{9,... | collective-permute-start | bytes 294920
  2190.1 135.1 %collective-permute-start.112 = (f32[16,1536]{1,0:T(8,128)S(1)}, f32[16,1536]{1,0:T(8,128)}, u32[]{:S(2)}, u32[]{:S(2)}) collective-permute-start(f32[16,1536]{1,0:T(8,128)S(1)} %get-tuple-element.26), channel_id=1, source_target_pairs={{0,17},{1,18},{2,19},{3,20},{4,21},{5,22},{6,23},{7,24},{8,25},{9,... | collective-permute-start | bytes 294920
  2192.0 137.2 %collective-permute-start.111 = (f32[16,1536]{1,0:T(8,128)S(1)}, f32[16,1536]{1,0:T(8,128)}, u32[]{:S(2)}, u32[]{:S(2)}) collective-permute-start(f32[16,1536]{1,0:T(8,128)S(1)} %get-tuple-element.26), channel_id=1, source_target_pairs={{0,16},{1,17},{2,18},{3,19},{4,20},{5,21},{6,22},{7,23},{8,24},{9,... | collective-permute-start | bytes 294920
  2337.7 50.3 %collective-permute-start.104 = (f32[16,1536]{1,0:T(8,128)S(1)}, f32[16,1536]{1,0:T(8,128)}, u32[]{:S(2)}, u32[]{:S(2)}) collective-permute-start(f32[16,1536]{1,0:T(8,128)S(1)} %get-tuple-element.26), channel_id=1, source_target_pairs={{0,9},{1,10},{2,11},{3,12},{4,13},{5,14},{6,15},{7,16},{8,17},{9,1... | collective-permute-start | bytes 294920
  (252 other events, 11176.3 us)
Sparse Core Ops, SparseCore 0:
  9.7 196.1 all-gather.23
  207.7 192.7 all-gather.25
  403.4 45.3 all-gather.13
  450.4 200.5 all-gather.27
  653.6 46.1 all-gather.15
  701.4 200.6 all-gather.29
  904.3 71.5 all-gather.19
  978.1 64.6 all-gather.17
  1045.1 78.2 all-gather.21
  1335.3 77.2 reduce-scatter.23
  1416.7 70.9 reduce-scatter.25
  1491.5 103.8 reduce-scatter.21
  1599.9 109.2 reduce-scatter.19
  1712.9 108.6 reduce-scatter.17
where the time goes:
time: 2460 us; the launch traced here: 2440 us
  waiting for transfers between devices  1140 us (46%)
  blocking collectives  496 us (20%)
  starting transfers between devices  396 us (16%)
  local copies, waits for them, and re-layouts  215 us (9%)
  matrix products  131 us (5%)
  other arithmetic  50.8 us (2%)
    unnamed x3, blocking collectives  496 us
    unnamed x130, starting transfers between devices  351 us
    all_gather x1, waiting for transfers between devices, shards(): lax.all_gather(w_query, ('seq', 'batch'), axis=0, tiled=True)  201 us
    all_gather x1, waiting for transfers between devices, shards(): lax.all_gather(w_out, ('seq', 'batch'), axis=0, tiled=True)  192 us
    all_gather x1, waiting for transfers between devices, shards(): lax.all_gather(w_key, ('seq', 'batch'), axis=0, tiled=True)  188 us
    unnamed x287, local copies, waits for them, and re-layouts  157 us
    unnamed x144, waiting for transfers between devices  135 us
    all_gather x1, waiting for transfers between devices, shards(): lax.all_gather(w_value, ('seq', 'batch'), axis=0, tiled=True)  127 us
  transfers between devices with their start and end apart: 146, of which 20 were waited for; matrix products, arithmetic and copies ran while one was open for 27% of the time, Pallas kernels for 0%

commit v1 on v0

v1 whole, which is shorter than its diff:
```python
import jax
import jax.numpy as jnp
from jax import lax
from jax.sharding import Mesh, PartitionSpec as P

HEAD_DIM = 64
TOPK = 8
GROUP = 3
Q_OWN = GROUP * HEAD_DIM
norm_eps = 1e-06
rope_base = 10000.0
masked_score = -1e30
SEQ = ("yh", "x")
BATCH = ("yl", "z", "c")
SIZE = {"yh": 2, "x": 4, "yl": 2, "z": 4, "c": 2}
bf16 = jnp.bfloat16
f32 = jnp.float32


def dot(a, b):
    return jnp.dot(a, b, preferred_element_type=f32)


def shift(value, axis, by):
    size = SIZE[axis]
    return lax.ppermute(value, axis, [(i, (i + by) % size) for i in range(size)])


def gather_ring(block, axis):
    half = block.shape[0] // 2
    below = shift(block, axis, 1)
    above = shift(block, axis, -1)
    low = shift(below[:half], axis, 1)
    high = shift(above[half:], axis, -1)
    return [block, above, jnp.concatenate([low, high], axis=0), below]


def gather_seq(block):
    other = shift(block, "yh", 1)
    return gather_ring(block, "x") + gather_ring(other, "x")


def add_low(*parts):
    total = parts[0].astype(f32)
    for part in parts[1:]:
        total = total + part.astype(f32)
    return total


def reduce_ring(blocks, axis):
    half = blocks[0].shape[0] // 2
    ahead = shift(blocks[2][:half], axis, 1)
    behind = shift(blocks[2][half:], axis, -1)
    up = jnp.concatenate(
        [add_low(blocks[1][:half], ahead).astype(bf16), blocks[1][half:].astype(bf16)], axis=0
    )
    down = jnp.concatenate(
        [blocks[3][:half].astype(bf16), add_low(blocks[3][half:], behind).astype(bf16)], axis=0
    )
    return add_low(blocks[0], shift(up, axis, 1), shift(down, axis, -1))


def reduce_seq(blocks):
    far = reduce_ring(blocks[4:], "x").astype(bf16)
    far = shift(far, "yh", 1)
    return add_low(reduce_ring(blocks[:4], "x"), far)


def reduce_batch(blocks):
    sent = shift(blocks[:, :, 1], "c", 1)
    held = add_low(blocks[:, :, 0], sent).astype(bf16)
    ring = [jnp.swapaxes(held[:, k], 0, 1) for k in range(4)]
    total = reduce_ring(ring, "z")
    total = jnp.swapaxes(total, 0, 1)
    return total[0] + shift(total[1].astype(bf16), "yl", 1).astype(f32)


def to_relative(value, axes):
    for place, axis in enumerate(axes):
        value = jnp.roll(value, -lax.axis_index(axis), axis=place)
    return value


def to_absolute(value, axes):
    for place, axis in enumerate(axes):
        value = jnp.roll(value, lax.axis_index(axis), axis=place)
    return value


def seq_relative(rows):
    shape = rows.shape
    return to_relative(rows.reshape((2, 4, shape[0] // 8) + shape[1:]), SEQ).reshape(shape)


def seq_absolute(rows):
    shape = rows.shape
    return to_absolute(rows.reshape((2, 4, shape[0] // 8) + shape[1:]), SEQ).reshape(shape)


def rms_scale(values):
    return lax.rsqrt(jnp.mean(values * values, axis=-1, keepdims=True) + norm_eps)


def rotate(values, cosine, sine):
    half_dim = values.shape[-1] // 2
    turned = jnp.concatenate([-values[..., half_dim:], values[..., :half_dim]], axis=-1)
    return values * cosine + turned * sine


def rope_tables(position):
    freq_index = jnp.arange(HEAD_DIM // 2, dtype=f32) * (2.0 / HEAD_DIM)
    frequency = rope_base ** (-freq_index)
    angle = position.astype(f32)[..., None] * frequency
    angle = jnp.concatenate([angle, angle], axis=-1)
    return (jnp.cos(angle), jnp.sin(angle))


def shards(
    tokens,
    cotangent,
    segments,
    routes,
    gate_weights,
    w_query,
    w_key,
    w_value,
    w_out,
    norm_one,
    norm_two,
    w_gate,
    w_up,
    w_down,
):
    rows = tokens.shape[1]
    features = tokens.shape[2]
    length = segments.shape[1]
    experts = 32
    capacity = rows * TOPK * 3 // (2 * experts)
    score_scale = HEAD_DIM ** (-0.5)
    wide = 384

    strip = jnp.concatenate([w_query, w_key, w_value, w_out], axis=1)
    strip = lax.all_gather(strip, BATCH, axis=0, tiled=True)
    gains = jnp.stack([norm_one, norm_two], axis=1)
    gains = lax.all_gather(gains, BATCH, axis=0, tiled=True)
    part = strip.shape[0]
    by_head = jnp.concatenate(
        [
            strip[:, :1536].reshape(part, 8, Q_OWN),
            strip[:, 1536:2048].reshape(part, 8, HEAD_DIM),
            strip[:, 2048:2560].reshape(part, 8, HEAD_DIM),
            jnp.broadcast_to(jnp.pad(gains, ((0, 0), (0, 62)))[:, None, :], (part, 8, 64)),
        ],
        axis=2,
    )
    by_head = lax.all_to_all(jnp.swapaxes(by_head, 0, 1), SEQ, 0, 0, tiled=True)
    by_head = by_head.reshape(features, wide)
    w_own = by_head[:, :320]
    w_out_own = strip[:, 2560:]
    gain_one = by_head[:, 320].astype(f32)
    gain_two = by_head[:, 321].astype(f32)

    gate_full = lax.all_gather(w_gate, SEQ, axis=1, tiled=True)
    up_full = lax.all_gather(w_up, SEQ, axis=1, tiled=True)
    down_full = lax.all_gather(w_down, SEQ, axis=1, tiled=True)

    flat = routes[0]
    expert_ids = jnp.arange(experts, dtype=jnp.int32)
    gate_dense = jnp.sum(
        jnp.where(flat[:, :, None] == expert_ids, gate_weights[0][:, :, None], 0.0), axis=1
    )
    gate_all = lax.all_gather(gate_dense, BATCH, axis=0)
    grad_all = lax.all_gather(cotangent[0], BATCH, axis=0)
    batch_index = lax.axis_index(BATCH)
    gate_own = lax.dynamic_slice_in_dim(gate_all, batch_index * 2, 2, axis=2)
    gate_own = jnp.transpose(gate_own, (2, 0, 1))
    hit = (gate_own > 0).astype(f32)
    slot = (jnp.cumsum(hit, axis=2) - 1.0) * hit - (1.0 - hit)
    select = (
        slot[:, :, None, :] == jnp.arange(capacity, dtype=f32)[None, None, :, None]
    )
    gate_slot = jnp.sum(jnp.where(select, gate_own[:, :, None, :], 0.0), axis=3)
    select = select.astype(bf16)

    inputs = tokens[0].astype(f32)
    upstream = cotangent[0].astype(f32)
    seq_rows = jnp.concatenate(gather_seq(tokens[0]), axis=0).astype(f32)
    scale_all = rms_scale(seq_rows)
    normed_one = (seq_rows * scale_all * gain_one).astype(bf16)
    raw = seq_absolute(dot(normed_one, w_own))
    seg = segments[0]
    place = jnp.arange(length, dtype=jnp.int32)
    earlier = jnp.sum((seg[None, :] < seg[:, None]).astype(jnp.int32), axis=1)
    cosine, sine = rope_tables(place - earlier)
    queries = rotate(
        raw[:, :Q_OWN].reshape(length, GROUP, HEAD_DIM), cosine[:, None], sine[:, None]
    ).astype(bf16)
    keys = rotate(raw[:, Q_OWN : Q_OWN + HEAD_DIM], cosine, sine).astype(bf16)
    values = raw[:, Q_OWN + HEAD_DIM :].astype(bf16)
    allowed = (seg[None, :] == seg[:, None]) & (place[None, :] <= place[:, None])
    scores = jnp.einsum("qgd,td->gqt", queries, keys, preferred_element_type=f32) * score_scale
    scores = jnp.where(allowed[None], scores, masked_score)
    row_max = jnp.max(scores, axis=-1, keepdims=True)
    exp_scores = jnp.exp(scores - row_max)
    denominator = jnp.sum(exp_scores, axis=-1, keepdims=True)
    soft = exp_scores / denominator
    soft_low = soft.astype(bf16)
    mixed = jnp.einsum("gqt,td->qgd", soft_low, values, preferred_element_type=f32)
    mixed = seq_relative(mixed.reshape(length, Q_OWN).astype(bf16))
    partial = dot(mixed, w_out_own).astype(bf16)
    hidden = inputs + reduce_seq([partial[k * rows : (k + 1) * rows] for k in range(8)])

    scale_two = rms_scale(hidden)
    normed_two = (hidden * scale_two * gain_two).astype(bf16)
    normed_all = lax.all_gather(normed_two, BATCH, axis=0)
    expert_in = jnp.einsum(
        "ebct,btd->ebcd", select, normed_all, preferred_element_type=f32
    ).astype(bf16)
    expert_in = expert_in.reshape(2, -1, features)
    grad_rows = jnp.einsum("ebct,btd->ebcd", select, grad_all, preferred_element_type=f32)
    grad_rows = (grad_rows * gate_slot[..., None]).astype(bf16).reshape(2, -1, features)
    gate_pre = jnp.einsum("ecd,edf->ecf", expert_in, gate_full, preferred_element_type=f32)
    up_pre = jnp.einsum("ecd,edf->ecf", expert_in, up_full, preferred_element_type=f32)
    sigmoid_gate = jax.nn.sigmoid(gate_pre)
    activated = (gate_pre * sigmoid_gate * up_pre).astype(bf16)
    grad_act = jnp.einsum("ecd,efd->ecf", grad_rows, down_full, preferred_element_type=f32)
    grad_gate_pre = (
        grad_act * up_pre * sigmoid_gate * (1.0 + gate_pre * (1.0 - sigmoid_gate))
    ).astype(bf16)
    grad_up_pre = (grad_act * gate_pre * sigmoid_gate).astype(bf16)
    grad_in = jnp.einsum("ecf,edf->ecd", grad_gate_pre, gate_full, preferred_element_type=f32)
    grad_in = grad_in + jnp.einsum(
        "ecf,edf->ecd", grad_up_pre, up_full, preferred_element_type=f32
    )
    grad_in = grad_in.astype(bf16).reshape(2, 16, capacity, features)
    grad_part = jnp.einsum("ebct,ebcd->btd", select, grad_in, preferred_element_type=f32)
    grad_part = to_relative(grad_part.astype(bf16).reshape(2, 4, 2, rows, features), BATCH)
    grad_normed_two = reduce_batch(grad_part)

    expert_out = jnp.einsum("ecf,efd->ecd", activated, down_full, preferred_element_type=f32)
    expert_out = expert_out.reshape(2, 16, capacity, features) * gate_slot[..., None]
    out_part = jnp.einsum(
        "ebct,ebcd->btd", select, expert_out.astype(bf16), preferred_element_type=f32
    )
    out_part = to_relative(out_part.astype(bf16).reshape(2, 4, 2, rows, features), BATCH)
    output = hidden + reduce_batch(out_part)

    grad_down = jnp.einsum("ecf,ecd->efd", activated, grad_rows, preferred_element_type=f32)
    grad_gate = jnp.einsum("ecd,ecf->edf", expert_in, grad_gate_pre, preferred_element_type=f32)
    grad_up = jnp.einsum("ecd,ecf->edf", expert_in, grad_up_pre, preferred_element_type=f32)

    def reduce_expert(grad):
        shape = grad.shape
        parts = grad.astype(bf16).reshape(2, 2, 4, shape[1] // 8, shape[2])
        parts = to_relative(jnp.transpose(parts, (1, 2, 0, 3, 4)), SEQ)
        parts = parts.reshape((8, 2, shape[1] // 8, shape[2]))
        return reduce_seq([parts[k] for k in range(8)])

    sum_down = reduce_expert(grad_down)
    sum_gate = reduce_expert(grad_gate)
    sum_up = reduce_expert(grad_up)

    scaled_two = gain_two * grad_normed_two
    grad_gain_two = jnp.sum(grad_normed_two * hidden * scale_two, axis=0)
    grad_hidden = (
        upstream
        + scale_two * scaled_two
        - hidden * scale_two**3 * jnp.mean(scaled_two * hidden, axis=-1, keepdims=True)
    )
    grad_z = jnp.concatenate(gather_seq(grad_hidden.astype(bf16)), axis=0)
    grad_mixed = jnp.einsum("td,fd->tf", grad_z, w_out_own, preferred_element_type=f32)
    grad_mixed = seq_absolute(grad_mixed.astype(bf16)).reshape(length, GROUP, HEAD_DIM)
    grad_out_w = dot(mixed.T, grad_z)
    grad_soft = jnp.einsum("qgd,td->gqt", grad_mixed, values, preferred_element_type=f32)
    row_dot = jnp.sum(soft * grad_soft, axis=-1, keepdims=True)
    grad_scores = (soft * (grad_soft - row_dot)).astype(bf16)
    grad_query = (
        jnp.einsum("gqt,td->qgd", grad_scores, keys, preferred_element_type=f32) * score_scale
    )
    grad_key = (
        jnp.einsum("gqt,qgd->td", grad_scores, queries, preferred_element_type=f32) * score_scale
    )
    grad_value = jnp.einsum("gqt,qgd->td", soft_low, grad_mixed, preferred_element_type=f32)
    grad_query = rotate(grad_query, cosine[:, None], -sine[:, None])
    grad_key = rotate(grad_key, cosine, -sine)
    grad_raw = jnp.concatenate(
        [grad_query.reshape(length, Q_OWN), grad_key, grad_value], axis=1
    ).astype(bf16)
    grad_raw = seq_relative(grad_raw)
    grad_normed_part = jnp.einsum("tf,df->td", grad_raw, w_own, preferred_element_type=f32)
    gain_one_part = jnp.sum(grad_normed_part * seq_rows * scale_all, axis=0)
    grad_normed_part = grad_normed_part.astype(bf16)
    grad_normed_one = reduce_seq([grad_normed_part[k * rows : (k + 1) * rows] for k in range(8)])
    scaled_one = gain_one * grad_normed_one
    scale_one = rms_scale(inputs)
    grad_inputs = (
        grad_hidden
        + scale_one * scaled_one
        - inputs * scale_one**3 * jnp.mean(scaled_one * inputs, axis=-1, keepdims=True)
    )

    grad_own = dot(normed_one.T, grad_raw)
    gain_cols = jnp.stack([gain_one_part, grad_gain_two], axis=1)
    grad_own = jnp.concatenate([grad_own, jnp.pad(gain_cols, ((0, 0), (0, 62)))], axis=1)
    grad_own = grad_own.astype(bf16).reshape(8, part, wide)
    grad_own = lax.all_to_all(grad_own, SEQ, 0, 0, tiled=True)
    grad_own = jnp.swapaxes(grad_own, 0, 1)
    gain_sum = jnp.sum(grad_own[:, :, 320:].astype(f32), axis=1).astype(bf16)
    grad_cols = jnp.concatenate(
        [
            grad_own[:, :, :Q_OWN].reshape(part, 1536),
            grad_own[:, :, Q_OWN : Q_OWN + HEAD_DIM].reshape(part, 512),
            grad_own[:, :, Q_OWN + HEAD_DIM : 320].reshape(part, 512),
            jnp.pad(gain_sum, ((0, 0), (0, 64))),
        ],
        axis=1,
    )

    def reduce_rows(grad):
        parts = grad.astype(bf16).reshape(2, 4, 2, part // 16, grad.shape[1])
        return reduce_batch(to_relative(parts, BATCH))

    sum_out = reduce_rows(grad_out_w)
    sums = reduce_rows(grad_cols)
    return (
        output.astype(bf16)[None],
        grad_inputs.astype(bf16)[None],
        sums[:, :1536],
        sums[:, 1536:2048],
        sums[:, 2048:2560],
        sum_out,
        sums[:, 2560],
        sums[:, 2561],
        sum_gate,
        sum_up,
        sum_down,
    )


def solution(mesh):
    fine = Mesh(mesh.devices.reshape(2, 4, 2, 4, 2), SEQ + BATCH)
    both = SEQ + BATCH
    placed = (
        P(BATCH, SEQ, None),
        P(BATCH, SEQ, None),
        P(BATCH, None),
        P(BATCH, SEQ, None),
        P(BATCH, SEQ, None),
        P(both, None),
        P(both, None),
        P(both, None),
        P(both, None),
        P(both),
        P(both),
        P(BATCH, SEQ, None),
        P(BATCH, SEQ, None),
        P(BATCH, SEQ, None),
    )
    return jax.shard_map(
        shards,
        mesh=fine,
        in_specs=placed,
        out_specs=(
            P(BATCH, SEQ, None),
            P(BATCH, SEQ, None),
            P(both, None),
            P(both, None),
            P(both, None),
            P(both, None),
            P(both),
            P(both),
            P(BATCH, SEQ, None),
            P(BATCH, SEQ, None),
            P(BATCH, SEQ, None),
        ),
        check_vma=False,
    )
```

time: 2460 us -> 808 us (0.33)
  waiting for transfers between devices: 1140 us -> 321 us
  blocking collectives: 496 us -> 40.1 us
  starting transfers between devices: 396 us -> 135 us
  local copies, waits for them, and re-layouts: 215 us -> 68.6 us
  other arithmetic: 50.8 us -> 117 us
  matrix products: 131 us -> 99.8 us
    all_gather x9 -> x6, waiting for transfers between devices: 795 us -> 170 us  [the longest x1 58.3 us: shards(): gate_full = lax.all_gather(w_gate, SEQ, axis=1, tiled=True)]
    unnamed x3 -> x0, blocking collectives: 496 us -> none
    unnamed x130 -> x0, starting transfers between devices: 351 us -> none
    all_to_all x4 -> x2, waiting for transfers between devices: 209 us -> 10.1 us  [the longest x1 10.1 us: shards(): by_head = lax.all_to_all(jnp.swapaxes(by_head, 0, 1), SEQ, 0, 0, tiled=True)]
    ppermute x0 -> x87, waiting for transfers between devices: none -> 139 us  [shift(): lax.ppermute(value, axis, [(i, (i + by) % size) for i in range(size)])]
    unnamed x287 -> x168, local copies, waits for them, and re-layouts: 157 us -> 22.1 us
    unnamed x144 -> x6, waiting for transfers between devices: 135 us -> 1.63 us
    ppermute x0 -> x87, starting transfers between devices: none -> 128 us  [shift(): lax.ppermute(value, axis, [(i, (i + by) % size) for i in range(size)])]
  transfers between devices with their start and end apart: 146 -> 95, of which waited for: 20 -> 43; matrix products, arithmetic and copies ran while one was open for 27% -> 27% of each run, Pallas kernels for 0% -> 0%
where the time goes in v1:
time: 808 us; the launch traced here: 798 us
  waiting for transfers between devices  321 us (40%)
  starting transfers between devices  135 us (17%)
  other arithmetic  117 us (14%)
  matrix products  99.8 us (12%)
  local copies, waits for them, and re-layouts  68.6 us (8%)
  blocking collectives  40.1 us (5%)
  between operations  16.6 us (2%)
    ppermute x87, waiting for transfers between devices, shift(): lax.ppermute(value, axis, [(i, (i + by) % size) for i in range(size)])  139 us
    ppermute x87, starting transfers between devices, shift(): lax.ppermute(value, axis, [(i, (i + by) % size) for i in range(size)])  128 us
    all_gather x1, waiting for transfers between devices, shards(): gate_full = lax.all_gather(w_gate, SEQ, axis=1, tiled=True)  58.3 us
    all_gather x1, waiting for transfers between devices, shards(): up_full = lax.all_gather(w_up, SEQ, axis=1, tiled=True)  56.1 us
    all_gather x1, waiting for transfers between devices, shards(): down_full = lax.all_gather(w_down, SEQ, axis=1, tiled=True)  55.9 us
    concatenate x20, other arithmetic, to_relative(): value = jnp.roll(value, -lax.axis_index(axis), axis=place)  37.5 us
    unnamed x168, local copies, waits for them, and re-layouts  22.1 us
    all_gather x1, blocking collectives, shards(): gains = lax.all_gather(gains, BATCH, axis=0, tiled=True)  20.6 us
  transfers between devices with their start and end apart: 95, of which 43 were waited for; matrix products, arithmetic and copies ran while one was open for 27% of the time, Pallas kernels for 0%

profile of v1, /device:TPU:8, one launch (start us, length us, event | category | flops | bytes accessed | tf_op | source)
XLA Modules:
  0.0 798.2 jit_solution(16889833560179407869)
XLA Ops:
  19.8 20.6 %all-gather.3 = bf16[16,12,2]{1,2,0:T(2,128)(2,1)S(1)} all-gather(bf16[1,12,2]{1,2,0:T(2,128)(2,1)S(1)} %maximum_bitcast_fusion.2), channel_id=1, replica_groups=mesh['yh'=2,'x'=4,'yl'=2,'z'=4,'c'=2] {'yl','z','c'}, dimensions={0}, use_global_device_ids=true | all-gather | bytes 816 | tf_op jit(solution)/shard_map/all_gather | solution.py:145
  92.2 10.1 %all-to-all-done = bf16[8,192,384]{2,1,0:T(8,128)(2,1)S(1)} async-done(((bf16[8,192,384]{2,1,0:T(8,128)(2,1)}), bf16[8,192,384]{2,1,0:T(8,128)(2,1)S(1)}, u32[]{:S(2)}, u32[]{:S(2)}) %all-to-all-start) | async-done | bytes 1179680 | tf_op jit(solution)/shard_map/all_to_all | solution.py:156
  118.0 5.7 fusion.64
  146.9 12.6 %collective-permute-start.12 = (bf16[128,1536]{1,0:T(8,128)(2,1)S(1)}, bf16[128,1536]{1,0:T(8,128)(2,1)S(1)}, u32[]{:S(2)}, u32[]{:S(2)}) collective-permute-start(bf16[128,1536]{1,0:T(8,128)(2,1)S(1)} %pad_maximum_fusion.6), channel_id=1, source_target_pairs={{0,48},{16,0},{32,16},{48,32},{1,49},{17,1},{33,17},{49,33},{2,50}... | collective-permute-start | bytes 1179656 | tf_op jit(solution)/shard_map/ppermute | solution.py:26
  173.8 19.4 %all-gather = f32[2048,32]{0,1:T(8,128)S(1)} all-gather(f32[128,32]{0,1:T(8,128)S(1)} %select_reduce_fusion.1), channel_id=2, replica_groups=mesh['yh'=2,'x'=4,'yl'=2,'z'=4,'c'=2] {'yl','z','c'}, dimensions={0}, use_global_device_ids=true | all-gather | bytes 278528 | tf_op jit(solution)/shard_map/all_gather | solution.py:172
  194.3 9.5 %fusion.2 = bf16[1024,3,1024]{2,0,1:T(8,128)(2,1)} fusion(f32[1024,1024,3]{1,0,2:T(8,128)} %copy-done, f32[3,1024]{1,0:T(4,128)S(1)} %fusion.8, f32[3,1024]{1,0:T(4,128)S(1)} %get-tuple-element.148, pred[1024,1024]{1,0:T(8,128)(4,1)S(1)} %copy-done.14), kind=kLoop, calls=%fused_computation.15 | loop fusion | flops 15728640 | bytes 19947520 | tf_op jit(solution)/shard_map/convert_element_type | solution.py:207
  217.2 58.3 %all-gather.11.cloned.1.call-done = bf16[2,1536,512]{2,1,0:T(8,128)(2,1)} async-done(((bf16[2,192,512]{2,1,0:T(8,128)(2,1)}), bf16[2,1536,512]{2,1,0:T(8,128)(2,1)}) %all-gather.11.cloned.1.call-update) | async-done | bytes 3145744 | tf_op jit(solution)/shard_map/all_gather | solution.py:163
  275.5 7.5 fusion.172
  283.0 56.1 %all-gather.13.cloned.1.call-done = bf16[2,1536,512]{2,1,0:T(8,128)(2,1)} async-done(((bf16[2,192,512]{2,1,0:T(8,128)(2,1)}), bf16[2,1536,512]{2,1,0:T(8,128)(2,1)}) %all-gather.13.cloned.1.call-update) | async-done | bytes 3145744 | tf_op jit(solution)/shard_map/all_gather | solution.py:164
  339.1 7.7 fusion.173
  346.8 55.9 %all-gather.15.cloned.1.call-done = bf16[2,512,1536]{2,1,0:T(8,128)(2,1)} async-done(((bf16[2,64,1536]{2,1,0:T(8,128)(2,1)}), bf16[2,512,1536]{2,1,0:T(8,128)(2,1)}) %all-gather.15.cloned.1.call-update) | async-done | bytes 3145744 | tf_op jit(solution)/shard_map/all_gather | solution.py:165
  402.7 9.0 %multiply_convert_fusion = (bf16[2,768,512]{2,1,0:T(8,128)(2,1)S(1)}, bf16[2,768,512]{2,1,0:T(8,128)(2,1)S(1)}, bf16[2,768,512]{2,1,0:T(8,128)(2,1)S(1)}) fusion(f32[2,768,512]{2,1,0:T(8,128)} %fusion.172, f32[2,768,512]{2,1,0:T(8,128)} %fusion.173, bf16[2,768,1536]{2,1,0:T(8,128)(2,1)} %bitcast.556, bf16[2,512,1536]{2,1,0:T(8,128)(2,1)} %all-gather.15.cloned.1.call-done), kind=kOutput, calls=%fused_computation.91 | convolution fusion | flops 2428502016 | bytes 18874368 | tf_op jit(solution)/shard_map/ecd,efd->ecf/dot_general | solution.py:226
  468.2 6.5 fusion.17
  543.1 6.3 collective-permute-done.19
  561.7 9.0 %collective-permute-done.20 = bf16[128,2,1536]{2,0,1:T(8,128)(2,1)S(1)} collective-permute-done((bf16[128,2,1536]{2,0,1:T(8,128)(2,1)S(1)}, bf16[128,2,1536]{2,0,1:T(8,128)(2,1)S(1)}, u32[]{:S(2)}, u32[]{:S(2)}) %collective-permute-start.20) | collective-permute-done | bytes 786464 | tf_op jit(solution)/shard_map/ppermute | solution.py:26
  576.2 10.3 %collective-permute-done.26 = bf16[128,2,1536]{2,0,1:T(8,128)(2,1)S(1)} collective-permute-done((bf16[128,2,1536]{2,0,1:T(8,128)(2,1)S(1)}, bf16[128,2,1536]{2,0,1:T(8,128)(2,1)S(1)}, u32[]{:S(2)}, u32[]{:S(2)}) %collective-permute-start.26) | collective-permute-done | bytes 786464 | tf_op jit(solution)/shard_map/ppermute | solution.py:26
  592.3 10.2 %collective-permute-done.86 = bf16[2,64,1536]{2,1,0:T(8,128)(2,1)S(1)} collective-permute-done((bf16[2,64,1536]{2,1,0:T(8,128)(2,1)S(1)}, bf16[2,64,1536]{2,1,0:T(8,128)(2,1)S(1)}, u32[]{:S(2)}, u32[]{:S(2)}) %collective-permute-start.86) | collective-permute-done | bytes 393248 | tf_op jit(solution)/shard_map/ppermute | solution.py:26
  607.0 6.5 collective-permute-done.29
  621.8 5.6 collective-permute-done.77
  640.9 8.0 %collective-permute-done.36 = bf16[128,1536]{1,0:T(8,128)(2,1)S(1)} collective-permute-done((bf16[128,1536]{1,0:T(8,128)(2,1)S(1)}, bf16[128,1536]{1,0:T(8,128)(2,1)S(1)}, u32[]{:S(2)}, u32[]{:S(2)}) %collective-permute-start.36) | collective-permute-done | bytes 393248 | tf_op jit(solution)/shard_map/ppermute | solution.py:26
  661.0 7.2 fusion.3
  668.3 7.2 fusion.5
  694.2 5.8 fusion.15
  745.4 9.7 %collective-permute-done.44 = bf16[128,1536]{1,0:T(8,128)(2,1)S(1)} collective-permute-done((bf16[128,1536]{1,0:T(8,128)(2,1)S(1)}, bf16[128,1536]{1,0:T(8,128)(2,1)S(1)}, u32[]{:S(2)}, u32[]{:S(2)}) %collective-permute-start.44) | collective-permute-done | bytes 393248 | tf_op jit(solution)/shard_map/ppermute | solution.py:26
  (583 shorter events, 416.7 us)
Async XLA Ops:
  7.2 59.8 %all-gather.21.cloned.1.call-start = ((), (), s32[]{:S(2)}) async-start(), calls=%async_computation.7 | async-start | bytes 2228224 | tf_op jit(solution)/shard_map/all_gather | solution.py:143
  8.8 195.0 %all-gather.17.cloned.1.call-start = ((), (), s32[]{:S(2)}) async-start(), calls=%async_computation.5 | async-start | bytes 6684672 | tf_op jit(solution)/shard_map/all_gather | solution.py:173
  8.9 36.2 %collective-permute-start = (bf16[128,1536]{1,0:T(8,128)(2,1)}, bf16[128,1536]{1,0:T(8,128)(2,1)S(1)}, u32[]{:S(2)}, u32[]{:S(2)}) collective-permute-start(bf16[128,1536]{1,0:T(8,128)(2,1)} %bitcast.546), channel_id=1, source_target_pairs={{0,48},{16,0},{32,16},{48,32},{1,49},{17,1},{33,17},{49,33},{2,50}... | collective-permute-start | bytes 1179656 | tf_op jit(solution)/shard_map/ppermute | solution.py:26
  11.7 32.5 %collective-permute-start.1 = (bf16[128,1536]{1,0:T(8,128)(2,1)}, bf16[128,1536]{1,0:T(8,128)(2,1)S(1)}, u32[]{:S(2)}, u32[]{:S(2)}) collective-permute-start(bf16[128,1536]{1,0:T(8,128)(2,1)} %bitcast.547), channel_id=1, source_target_pairs={{0,16},{16,32},{32,48},{48,0},{1,17},{17,33},{33,49},{49,1},{2,18}... | collective-permute-start | bytes 1179656 | tf_op jit(solution)/shard_map/ppermute | solution.py:26
  11.7 35.9 %collective-permute-start.4 = (bf16[128,1536]{1,0:T(8,128)(2,1)}, bf16[128,1536]{1,0:T(8,128)(2,1)}, u32[]{:S(2)}, u32[]{:S(2)}) collective-permute-start(bf16[128,1536]{1,0:T(8,128)(2,1)} %bitcast.548), channel_id=1, source_target_pairs={{0,64},{64,0},{1,65},{65,1},{2,66},{66,2},{3,67},{67,3},{4,68},{68... | collective-permute-start | bytes 1179656 | tf_op jit(solution)/shard_map/ppermute | solution.py:26
  85.2 125.4 %all-gather.19.cloned.1.call-start = ((), (), s32[]{:S(2)}) async-start(), calls=%async_computation.6 | async-start | bytes 6684672 | tf_op jit(solution)/shard_map/all_gather | solution.py:215
  172.0 103.5 %all-gather.11.cloned.1.call-start = ((), (), s32[]{:S(2)}) async-start(), calls=%async_computation.2 | async-start | bytes 3538944 | tf_op jit(solution)/shard_map/all_gather | solution.py:163
  172.5 166.6 %all-gather.13.cloned.1.call-start = ((), (), s32[]{:S(2)}) async-start(), calls=%async_computation.3 | async-start | bytes 3538944 | tf_op jit(solution)/shard_map/all_gather | solution.py:164
  173.1 229.6 %all-gather.15.cloned.1.call-start = ((), (), s32[]{:S(2)}) async-start(), calls=%async_computation.4 | async-start | bytes 3538944 | tf_op jit(solution)/shard_map/all_gather | solution.py:165
  420.4 77.7 %collective-permute-start.78 = (bf16[1,64,1536]{2,1,0:T(8,128)(2,1)}, bf16[1,64,1536]{2,1,0:T(8,128)(2,1)}, u32[]{:S(2)}, u32[]{:S(2)}) collective-permute-start(bf16[1,64,1536]{2,1,0:T(8,128)(2,1)} %get-tuple-element.44), channel_id=1, source_target_pairs={{0,16},{16,32},{32,48},{48,0},{1,17},{17,33},{33,49},{49,1},{2,18}... | collective-permute-start | bytes 589832 | tf_op jit(solution)/shard_map/ppermute | solution.py:26
  433.0 51.9 %collective-permute-start.69 = (bf16[1,192,512]{2,1,0:T(8,128)(2,1)}, bf16[1,192,512]{2,1,0:T(8,128)(2,1)}, u32[]{:S(2)}, u32[]{:S(2)}) collective-permute-start(bf16[1,192,512]{2,1,0:T(8,128)(2,1)} %get-tuple-element.56), channel_id=1, source_target_pairs={{0,16},{16,32},{32,48},{48,0},{1,17},{17,33},{33,49},{49,1},{2,18}... | collective-permute-start | bytes 589832 | tf_op jit(solution)/shard_map/ppermute | solution.py:26
  433.6 51.3 %collective-permute-start.71 = (bf16[1,192,512]{2,1,0:T(8,128)(2,1)}, bf16[1,192,512]{2,1,0:T(8,128)(2,1)}, u32[]{:S(2)}, u32[]{:S(2)}) collective-permute-start(bf16[1,192,512]{2,1,0:T(8,128)(2,1)} %get-tuple-element.61), channel_id=1, source_target_pairs={{0,48},{16,0},{32,16},{48,32},{1,49},{17,1},{33,17},{49,33},{2,50}... | collective-permute-start | bytes 589832 | tf_op jit(solution)/shard_map/ppermute | solution.py:26
  436.2 52.0 %collective-permute-start.73 = (bf16[1,192,512]{2,1,0:T(8,128)(2,1)}, bf16[1,192,512]{2,1,0:T(8,128)(2,1)}, u32[]{:S(2)}, u32[]{:S(2)}) collective-permute-start(bf16[1,192,512]{2,1,0:T(8,128)(2,1)} %get-tuple-element.60), channel_id=1, source_target_pairs={{0,16},{16,32},{32,48},{48,0},{1,17},{17,33},{33,49},{49,1},{2,18}... | collective-permute-start | bytes 589832 | tf_op jit(solution)/shard_map/ppermute | solution.py:26
  436.2 52.0 %collective-permute-start.75 = (bf16[1,192,512]{2,1,0:T(8,128)(2,1)}, bf16[1,192,512]{2,1,0:T(8,128)(2,1)}, u32[]{:S(2)}, u32[]{:S(2)}) collective-permute-start(bf16[1,192,512]{2,1,0:T(8,128)(2,1)} %get-tuple-element.57), channel_id=1, source_target_pairs={{0,48},{16,0},{32,16},{48,32},{1,49},{17,1},{33,17},{49,33},{2,50}... | collective-permute-start | bytes 589832 | tf_op jit(solution)/shard_map/ppermute | solution.py:26
  497.7 36.6 %collective-permute-start.18 = (bf16[2,4,128,1536]{3,2,0,1:T(8,128)(2,1)S(1)}, bf16[2,4,128,1536]{3,2,0,1:T(8,128)(2,1)S(1)}, u32[]{:S(2)}, u32[]{:S(2)}) collective-permute-start(bf16[2,4,128,1536]{3,2,0,1:T(8,128)(2,1)S(1)} %slice_bitcast_fusion.2), channel_id=1, source_target_pairs={{0,1},{1,0},{2,3},{3,2},{4,5},{5,4},{6,7},{7,6},{8,9},{9,8},{10,11... | collective-permute-start | bytes 9437192 | tf_op jit(solution)/shard_map/ppermute | solution.py:26
  498.1 41.6 %collective-permute-start.24 = (bf16[2,4,128,1536]{3,2,0,1:T(8,128)(2,1)S(1)}, bf16[2,4,128,1536]{3,2,0,1:T(8,128)(2,1)}, u32[]{:S(2)}, u32[]{:S(2)}) collective-permute-start(bf16[2,4,128,1536]{3,2,0,1:T(8,128)(2,1)S(1)} %slice_bitcast_fusion), channel_id=1, source_target_pairs={{0,1},{1,0},{2,3},{3,2},{4,5},{5,4},{6,7},{7,6},{8,9},{9,8},{10,11... | collective-permute-start | bytes 9437192 | tf_op jit(solution)/shard_map/ppermute | solution.py:26
  525.9 64.9 %collective-permute-start.79 = (bf16[2,64,1536]{2,1,0:T(8,128)(2,1)}, bf16[2,64,1536]{2,1,0:T(8,128)(2,1)S(1)}, u32[]{:S(2)}, u32[]{:S(2)}) collective-permute-start(bf16[2,64,1536]{2,1,0:T(8,128)(2,1)} %pad_maximum_fusion.21), channel_id=1, source_target_pairs={{0,16},{16,32},{32,48},{48,0},{1,17},{17,33},{33,49},{49,1},{2,18}... | collective-permute-start | bytes 1179656 | tf_op jit(solution)/shard_map/ppermute | solution.py:26
  531.4 60.4 %collective-permute-start.81 = (bf16[2,64,1536]{2,1,0:T(8,128)(2,1)}, bf16[2,64,1536]{2,1,0:T(8,128)(2,1)}, u32[]{:S(2)}, u32[]{:S(2)}) collective-permute-start(bf16[2,64,1536]{2,1,0:T(8,128)(2,1)} %pad_maximum_fusion.22), channel_id=1, source_target_pairs={{0,48},{16,0},{32,16},{48,32},{1,49},{17,1},{33,17},{49,33},{2,50}... | collective-permute-start | bytes 1179656 | tf_op jit(solution)/shard_map/ppermute | solution.py:26
  561.5 57.0 %collective-permute-start.70 = (bf16[2,192,512]{2,1,0:T(8,128)(2,1)S(1)}, bf16[2,192,512]{2,1,0:T(8,128)(2,1)S(1)}, u32[]{:S(2)}, u32[]{:S(2)}) collective-permute-start(bf16[2,192,512]{2,1,0:T(8,128)(2,1)S(1)} %copy-done.49), channel_id=1, source_target_pairs={{0,16},{16,32},{32,48},{48,0},{1,17},{17,33},{33,49},{49,1},{2,18}... | collective-permute-start | bytes 1179656 | tf_op jit(solution)/shard_map/ppermute | solution.py:26
  586.5 33.3 %collective-permute-start.72 = (bf16[2,192,512]{2,1,0:T(8,128)(2,1)S(1)}, bf16[2,192,512]{2,1,0:T(8,128)(2,1)S(1)}, u32[]{:S(2)}, u32[]{:S(2)}) collective-permute-start(bf16[2,192,512]{2,1,0:T(8,128)(2,1)S(1)} %copy-done.47), channel_id=1, source_target_pairs={{0,48},{16,0},{32,16},{48,32},{1,49},{17,1},{33,17},{49,33},{2,50}... | collective-permute-start | bytes 1179656 | tf_op jit(solution)/shard_map/ppermute | solution.py:26
  694.2 35.7 %collective-permute-start.54 = (bf16[2,4,12,1536]{3,2,1,0:T(8,128)(2,1)}, bf16[2,4,12,1536]{3,2,1,0:T(8,128)(2,1)}, u32[]{:S(2)}, u32[]{:S(2)}) collective-permute-start(bf16[2,4,12,1536]{3,2,1,0:T(8,128)(2,1)} %slice_bitcast_fusion.22), channel_id=1, source_target_pairs={{0,1},{1,0},{2,3},{3,2},{4,5},{5,4},{6,7},{7,6},{8,9},{9,8},{10,11... | collective-permute-start | bytes 884744 | tf_op jit(solution)/shard_map/ppermute | solution.py:26
  718.4 41.8 %all-to-all-start.1 = ((bf16[8,192,384]{2,1,0:T(8,128)(2,1)}), bf16[8,192,384]{2,1,0:T(8,128)(2,1)S(1)}, u32[]{:S(2)}, u32[]{:S(2)}) async-start(bf16[8,192,384]{2,1,0:T(8,128)(2,1)} %pad_maximum_fusion), calls=%async_computation.1 | async-start | bytes 2359296 | tf_op jit(solution)/shard_map/all_to_all | solution.py:306
  725.8 43.6 %collective-permute-start.40 = (bf16[128,1536]{1,0:T(8,128)(2,1)}, bf16[128,1536]{1,0:T(8,128)(2,1)S(1)}, u32[]{:S(2)}, u32[]{:S(2)}) collective-permute-start(bf16[128,1536]{1,0:T(8,128)(2,1)} %pad_maximum_fusion.9), channel_id=1, source_target_pairs={{0,16},{16,32},{32,48},{48,0},{1,17},{17,33},{33,49},{49,1},{2,18}... | collective-permute-start | bytes 1179656 | tf_op jit(solution)/shard_map/ppermute | solution.py:26
  728.6 40.9 %collective-permute-start.42 = (bf16[128,1536]{1,0:T(8,128)(2,1)}, bf16[128,1536]{1,0:T(8,128)(2,1)S(1)}, u32[]{:S(2)}, u32[]{:S(2)}) collective-permute-start(bf16[128,1536]{1,0:T(8,128)(2,1)} %pad_maximum_fusion.10), channel_id=1, source_target_pairs={{0,48},{16,0},{32,16},{48,32},{1,49},{17,1},{33,17},{49,33},{2,50}... | collective-permute-start | bytes 1179656 | tf_op jit(solution)/shard_map/ppermute | solution.py:26
  (144 other events, 1708.3 us)
Sparse Core Ops, SparseCore 0:
  10.3 36.6 all-gather.20
  48.7 53.0 all-gather.16
  172.1 38.4 all-gather.18
  212.7 62.7 all-gather.10
  277.6 61.4 all-gather.12
  341.2 61.4 all-gather.14

commit v2 on v1

v2 whole, which is shorter than its diff:
```python
import jax
import jax.numpy as jnp
from jax import lax
from jax.experimental import pallas as pl
from jax.experimental.pallas import tpu as pltpu
from jax.sharding import Mesh, PartitionSpec as P

HEAD_DIM = 64
TOPK = 8
GROUP = 3
Q_OWN = GROUP * HEAD_DIM
TOK = 128
HALF = 512
D = 1536
EXPERTS = 32
norm_eps = 1e-06
rope_base = 10000.0
masked_score = -1e30
SEQ = ("yh", "x")
BATCH = ("yl", "z", "c")
SIZE = {"yh": 2, "x": 4, "yl": 2, "z": 4, "c": 2}
bf16 = jnp.bfloat16
f32 = jnp.float32


def dot(a, b):
    return jnp.dot(a, b, preferred_element_type=f32)


def shift(value, axis, by):
    size = SIZE[axis]
    return lax.ppermute(value, axis, [(i, (i + by) % size) for i in range(size)])


def ring_pieces(block, axis):
    half = block.shape[0] // 2
    below = shift(block, axis, 1)
    above = shift(block, axis, -1)
    low = shift(below[:half], axis, 1)
    high = shift(above[half:], axis, -1)
    return block, above, low, high, below


def add_up(*parts):
    total = parts[0].astype(f32)
    for part in parts[1:]:
        total = total + part.astype(f32)
    return total


def ring_send(blocks, axis):
    half = blocks[0].shape[0] // 2
    return shift(blocks[2][:half], axis, 1), shift(blocks[2][half:], axis, -1)


def ring_add(blocks, got):
    half = blocks[0].shape[0] // 2
    up = [add_up(blocks[1][:half], got[0]).astype(bf16), blocks[1][half:]]
    down = [blocks[3][:half], add_up(blocks[3][half:], got[1]).astype(bf16)]
    return jnp.concatenate(up, axis=0), jnp.concatenate(down, axis=0)


def ring_next(hops, axis):
    return shift(hops[0], axis, 1), shift(hops[1], axis, -1)


def reduce_ring(blocks, axis):
    hops = ring_add(blocks, ring_send(blocks, axis))
    return add_up(blocks[0], *ring_next(hops, axis))


def reduce_plane(blocks, ring, pair):
    total = reduce_ring(blocks, ring)
    return add_up(total[0], shift(total[1].astype(bf16), pair, 1))


def reduce_batch(near, across):
    held = add_up(near, shift(across, "c", 1)).astype(bf16)
    return reduce_plane(held.reshape((4, 2) + near.shape[1:]), "z", "yl")


def tie(*values):
    return lax.optimization_barrier(values)


def ahead(axis, by):
    return lax.rem(lax.axis_index(axis) + by, SIZE[axis])


def distance(axis, place):
    return lax.rem(place - lax.axis_index(axis) + SIZE[axis], SIZE[axis])


def dot_nt(a, b):
    return lax.dot_general(a, b, (((1,), (1,)), ((), ())), preferred_element_type=f32)


def dot_tn(a, b):
    return lax.dot_general(a, b, (((0,), (0,)), ((), ())), preferred_element_type=f32)


def whole(shape):
    zeros = (0,) * len(shape)
    return pl.BlockSpec(shape, lambda *_: zeros)


def once(shape):
    zeros = (0,) * len(shape)
    return pl.BlockSpec(shape, lambda *_: zeros, pipeline_mode=pl.Buffered(1))


def run(body, out_shapes, in_specs, out_specs, grid, args, prefetch=None, scratch=(), micros=0):
    spec = pltpu.PrefetchScalarGridSpec(
        num_scalar_prefetch=0 if prefetch is None else 1,
        grid=grid,
        in_specs=in_specs,
        out_specs=out_specs,
        scratch_shapes=list(scratch),
    )
    head = () if prefetch is None else (prefetch,)
    return pl.pallas_call(
        body,
        grid_spec=spec,
        out_shape=out_shapes,
        compiler_params=pltpu.CompilerParams(vmem_limit_bytes=56 << 20),
        cost_estimate=pl.CostEstimate(flops=1100000000 * micros, bytes_accessed=0, transcendentals=0),
    )(*head, *args)


def struct(shape, dtype):
    return jax.ShapeDtypeStruct(shape, dtype)


def turned(values):
    lane = lax.broadcasted_iota(jnp.int32, values.shape, 1)
    first = (lane % HEAD_DIM) < HEAD_DIM // 2
    return jnp.where(first, -pltpu.roll(values, 96, 1), pltpu.roll(values, 32, 1))


def by_lanes(values, function):
    width = values.shape[1]
    return jnp.concatenate(
        [function(values[:, k : k + 128]) for k in range(0, width, 128)], axis=1
    )


def prepare_body(where, own, above, far_low, far_high, below, moving, xp_ref, scale_ref):
    for k in range(4):
        place = pl.ds(lax.rem(where[0] + k, 4) * TOK, TOK)
        if k == 2:
            block = jnp.concatenate([far_low[...], far_high[...]], axis=0)
        else:
            block = (own, above, None, below)[k][...]
        wide = block.astype(f32)
        scale = lax.rsqrt(jnp.mean(wide * wide, axis=1, keepdims=True) + norm_eps)
        scale_ref[place, :] = jnp.broadcast_to(scale, (TOK, 128))
        xp_ref[place, :] = dot(block, moving[...]).astype(bf16)


def prepare(where, pieces, moving):
    specs = [whole(p.shape) for p in pieces] + [whole(moving.shape)]
    return run(
        prepare_body,
        [struct((HALF, D), bf16), struct((HALF, 128), f32)],
        specs,
        [whole((HALF, D)), whole((HALF, 128))],
        (1,),
        (*pieces, moving),
        prefetch=where,
        micros=7,
    )


def project_body(xp, scale, weight, cosine, sine, n_ref, q_ref, kv_ref, sent_ref):
    pick = lax.broadcasted_iota(jnp.int32, (8, 128), 0) == lax.broadcasted_iota(
        jnp.int32, (8, 128), 1
    )
    gains = dot_nt(pick.astype(bf16), weight[:, 640:])
    normed = (xp[...].astype(f32) * scale[:, :1] * gains[:1]).astype(bf16)
    n_ref[...] = normed
    raw = dot(normed, weight[:, :640])
    cos, sin = cosine[...], sine[...]
    rotated = by_lanes(raw[:, :512], lambda u: u * cos + turned(u) * sin).astype(bf16)
    q_ref[...] = rotated[:, :384]
    both = jnp.concatenate([rotated[:, 384:], raw[:, 512:].astype(bf16)], axis=1)
    kv_ref[...] = both
    sent_ref[...] = swap_groups(both)


def swap_groups(both):
    wide = both.astype(f32)
    return by_lanes(wide, lambda u: pltpu.roll(u, 64, 1)).astype(bf16)


def tile(width):
    return pl.BlockSpec((TOK, width), lambda i, *_: (i, 0))


def project(xp, scale, gathered, cosine, sine):
    return run(
        project_body,
        [
            struct((HALF, D), bf16),
            struct((HALF, 384), bf16),
            struct((HALF, 256), bf16),
            struct((HALF, 256), bf16),
        ],
        [whole((HALF, D)), whole((HALF, 128)), whole((D, 768)), whole((HALF, 128)), whole((HALF, 128))],
        [whole((HALF, D)), whole((HALF, 384)), whole((HALF, 256)), whole((HALF, 256))],
        (1,),
        (xp, scale, gathered, cosine, sine),
        micros=5,
    )


def softmax_parts(where, step, q, own, other, seg_col, seg_row, group):
    place = lax.rem(where[0] + step, 4) * TOK
    row = lax.broadcasted_iota(jnp.int32, (TOK, HALF), 0) + place
    key = lax.broadcasted_iota(jnp.int32, (TOK, HALF), 1)
    segs = seg_col[:, :1]
    own_ok = (segs == seg_row[:, :HALF]) & (key <= row)
    other_ok = (segs == seg_row[:, HALF:]) & (where[1] == 1)
    first = group * HEAD_DIM
    heads = [q[:, (3 * group + h) * HEAD_DIM : (3 * group + h + 1) * HEAD_DIM] for h in range(3)]
    queries = jnp.concatenate(heads, axis=0) * jnp.asarray(0.125, bf16)
    scores = []
    for kv, ok in ((own, own_ok), (other, other_ok)):
        s = dot_nt(queries, kv[:, first : first + HEAD_DIM]).reshape(3, TOK, HALF)
        scores.append(jnp.where(ok[None], s, masked_score))
    top = jnp.maximum(
        jnp.max(scores[0], axis=2, keepdims=True), jnp.max(scores[1], axis=2, keepdims=True)
    )
    exps = [jnp.exp(s - top) for s in scores]
    total = jnp.sum(exps[0], axis=2, keepdims=True) + jnp.sum(exps[1], axis=2, keepdims=True)
    inverse = 1.0 / total
    return queries, [(e * inverse).reshape(3 * TOK, HALF) for e in exps]


def attend_body(where, q, own, other, seg_col, seg_row, w_own, w_other, att_ref, part_ref):
    step = pl.program_id(0)
    columns = []
    for group in range(2):
        _, probs = softmax_parts(where, step, q[...], own, other, seg_col, seg_row, group)
        first = 128 + group * HEAD_DIM
        mixed = dot(probs[0].astype(bf16), own[:, first : first + HEAD_DIM])
        mixed = mixed + dot(probs[1].astype(bf16), other[:, first : first + HEAD_DIM])
        columns += [mixed[h * TOK : (h + 1) * TOK] for h in range(3)]
    att = jnp.concatenate(columns, axis=1).astype(bf16)
    att_ref[...] = att
    part = dot(att[:, :Q_OWN], w_own[...]) + dot(att[:, Q_OWN:], w_other[...])
    part_ref[0] = part.astype(bf16)


def turn(width):
    return pl.BlockSpec((TOK, width), lambda i, where: (lax.rem(where[0] + i, 4), 0))


def step_block(shape):
    return pl.BlockSpec((1,) + shape, lambda i, *_: (i, 0, 0))


def attend(where, q, own, other, seg_col, seg_row, w_own, w_other):
    return run(
        attend_body,
        [struct((HALF, 384), bf16), struct((4, TOK, D), bf16)],
        [
            turn(384),
            whole((HALF, 256)),
            whole((HALF, 256)),
            turn(128),
            whole((1, 2 * HALF)),
            whole((Q_OWN, D)),
            whole((Q_OWN, D)),
        ],
        [turn(384), step_block((TOK, D))],
        (4,),
        (q, own, other, seg_col, seg_row, w_own, w_other),
        prefetch=where,
        micros=15,
    )


def attend_back_body(
    where, q, att, own, other, seg_col, seg_row, w_own, w_other, z0, z1, z2a, z2b, z3, cosine,
    sine, q_ref, own_ref, sent_ref, out_ref, sums, out_sum, z,
):
    step = pl.program_id(0)
    for k, pieces in enumerate(((z0,), (z1,), (z2a, z2b), (z3,))):

        @pl.when(step == k)
        def _(pieces=pieces):
            rows = TOK // len(pieces)
            for n, piece in enumerate(pieces):
                z[n * rows : (n + 1) * rows, :] = piece[...]

    @pl.when(step == 0)
    def _():
        sums[...] = jnp.zeros_like(sums)
        out_sum[...] = jnp.zeros_like(out_sum)

    place = pl.ds(lax.rem(where[0] + step, 4) * TOK, TOK)
    grad_z = z[...]
    out_sum[...] += dot_tn(att[...], grad_z)
    grad_att = jnp.concatenate([dot_nt(grad_z, w_own[...]), dot_nt(grad_z, w_other[...])], axis=1)
    grad_att = grad_att.astype(bf16)
    columns, keys, values = [], [[], []], [[], []]
    for group in range(2):
        queries, probs = softmax_parts(where, step, q[...], own, other, seg_col, seg_row, group)
        grads = jnp.concatenate(
            [
                grad_att[:, (3 * group + h) * HEAD_DIM : (3 * group + h + 1) * HEAD_DIM]
                for h in range(3)
            ],
            axis=0,
        )
        first = group * HEAD_DIM
        grad_probs = [dot_nt(grads, kv[:, 128 + first : 192 + first]) for kv in (own, other)]
        row_dot = jnp.sum(probs[0] * grad_probs[0], axis=1, keepdims=True)
        row_dot = row_dot + jnp.sum(probs[1] * grad_probs[1], axis=1, keepdims=True)
        total = None
        for n, kv in enumerate((own, other)):
            grad_score = (probs[n] * (grad_probs[n] - row_dot)).astype(bf16)
            term = dot(grad_score, kv[:, first : first + HEAD_DIM])
            total = term if total is None else total + term
            keys[n].append(dot_tn(grad_score, queries))
            values[n].append(dot_tn(probs[n].astype(bf16), grads))
        total = total * 0.125
        columns += [total[h * TOK : (h + 1) * TOK] for h in range(3)]
    for n in range(2):
        sums[n] += jnp.concatenate(keys[n] + values[n], axis=1)
    grad_q = jnp.concatenate(columns, axis=1)
    cos, sin = cosine[place, :], sine[place, :]
    q_ref[...] = by_lanes(grad_q, lambda u: u * cos - turned(u) * sin).astype(bf16)

    @pl.when(step == 3)
    def _():
        out_ref[...] = out_sum[...].astype(bf16)
        for n in range(2):
            at = slice(n * HALF, (n + 1) * HALF)
            grad_k = sums[n, :, :128]
            grad_k = grad_k * cosine[at, :] - turned(grad_k) * sine[at, :]
            both = jnp.concatenate([grad_k, sums[n, :, 128:]], axis=1)
            if n == 0:
                own_ref[...] = both
            else:
                sent_ref[...] = swap_groups(both)


def attend_back(where, q, att, own, other, seg_col, seg_row, w_own, w_other, pieces, cosine, sine):
    return run(
        attend_back_body,
        [
            struct((HALF, 384), bf16),
            struct((HALF, 256), f32),
            struct((HALF, 256), bf16),
            struct((384, D), bf16),
        ],
        [
            turn(384),
            turn(384),
            whole((HALF, 256)),
            whole((HALF, 256)),
            turn(128),
            whole((1, 2 * HALF)),
            whole((Q_OWN, D)),
            whole((Q_OWN, D)),
        ]
        + [whole(p.shape) for p in pieces]
        + [whole((2 * HALF, 128)), whole((2 * HALF, 128))],
        [turn(384), whole((HALF, 256)), whole((HALF, 256)), whole((384, D))],
        (4,),
        (q, att, own, other, seg_col, seg_row, w_own, w_other, *pieces, cosine, sine),
        prefetch=where,
        scratch=[
            pltpu.VMEM((2, HALF, 256), f32),
            pltpu.VMEM((384, D), f32),
            pltpu.VMEM((TOK, D), bf16),
        ],
        micros=22,
    )


def unproject_body(where, q, own, got, weight, moving, xp, scale, raw_ref, part_ref, gain_ref):
    both = (own[...] + got[...].astype(f32)).astype(bf16)
    raw = jnp.concatenate([q[...], both], axis=1)
    raw_ref[...] = raw
    grad = dot_nt(raw, weight[:, :640])
    term = jnp.sum(grad * (xp[...].astype(f32) * scale[:, :1]), axis=0, keepdims=True)
    gain_ref[...] = jnp.broadcast_to(term, (8, D))
    part = dot_nt(grad.astype(bf16), moving[...]).astype(bf16)
    for k in range(4):
        part_ref[lax.rem(k + 4 - where[0], 4)] = part[k * TOK : (k + 1) * TOK]


def unproject(where, q, own, got, gathered, moving, xp, scale):
    return run(
        unproject_body,
        [struct((HALF, 640), bf16), struct((4, TOK, D), bf16), struct((8, D), f32)],
        [
            whole((HALF, 384)),
            whole((HALF, 256)),
            whole((HALF, 256)),
            whole((D, 768)),
            whole((D, D)),
            whole((HALF, D)),
            whole((HALF, 128)),
        ],
        [whole((HALF, 640)), whole((4, TOK, D)), whole((8, D))],
        (1,),
        (q, own, got, gathered, moving, xp, scale),
        prefetch=where,
        micros=10,
    )


def weight_grad_body(order, normed, raw, gains, out_rows, out_ref):
    step = pl.program_id(0)
    grad = dot_tn(normed[...], raw[...]).astype(bf16)
    pick = lax.broadcasted_iota(jnp.int32, (8, 128), 0) == lax.broadcasted_iota(
        jnp.int32, (8, 128), 1
    )
    columns = dot_tn(gains[...].astype(bf16), pick.astype(bf16)).astype(bf16)
    for k in range(4):
        at = slice(k * 96, (k + 1) * 96)
        to = order[step * 4 + k]
        out_ref[to, :, :640] = grad[at]
        out_ref[to, :, 640:768] = columns[at]
        out_ref[to, :, 768:] = out_rows[k]


def weight_grad(order, normed, raw, gains, out_rows):
    return run(
        weight_grad_body,
        [struct((16, 96, 1152), bf16)],
        [
            pl.BlockSpec((HALF, 384), lambda i, *_: (0, i)),
            whole((HALF, 640)),
            pl.BlockSpec((8, 384), lambda i, *_: (0, i)),
            pl.BlockSpec((4, 96, 384), lambda i, *_: (i, 0, 0)),
        ],
        [whole((16, 96, 1152))],
        (4,),
        (normed, raw, gains, out_rows),
        prefetch=order,
        micros=6,
    )[0]


CAP = 48
BLOCKS = 8
NEAR = BLOCKS // 2
STEP = BLOCKS * CAP


def choices(gates):
    hit = gates > 0
    upper = lax.broadcasted_iota(jnp.int32, (TOK, TOK), 0) <= lax.broadcasted_iota(
        jnp.int32, (TOK, TOK), 1
    )
    count = dot(hit.astype(bf16), upper.astype(bf16))
    slot = lax.broadcasted_iota(jnp.int32, (CAP, TOK), 0).astype(f32) + 1.0
    picks, weights = [], []
    for e in range(2):
        pick = (count[e : e + 1] == slot) & hit[e : e + 1]
        picks.append(pick.astype(bf16))
        weights.append(jnp.sum(jnp.where(pick, gates[e : e + 1], 0.0), axis=1, keepdims=True))
    return jnp.concatenate(picks, axis=0), jnp.concatenate(weights, axis=0)


def experts_body(order, *refs):
    rows, grads, gates = (refs[k * BLOCKS : (k + 1) * BLOCKS] for k in range(3))
    w_gate, w_up, w_down = refs[3 * BLOCKS : 3 * BLOCKS + 3]
    near_ref, across_ref, in_ref, grad_ref, act_ref, da_ref, db_ref = refs[3 * BLOCKS + 3 :]
    picks = []
    for j in range(BLOCKS):
        pick, weight = choices(gates[j][0])
        picks.append(pick)
        taken = dot(pick, rows[j][0]).astype(bf16)
        graded = (dot(pick, grads[j][0]) * weight).astype(bf16)
        for e in range(2):
            at = slice(j * CAP, (j + 1) * CAP)
            in_ref[e, at, :] = taken[e * CAP : (e + 1) * CAP]
            grad_ref[e, at, :] = graded[e * CAP : (e + 1) * CAP]
    backs = []
    for e in range(2):
        taken, graded = in_ref[e], grad_ref[e]
        gate_pre = dot(taken, w_gate[e])
        up_pre = dot(taken, w_up[e])
        grad_act = dot_nt(graded, w_down[e])
        sig = 1.0 / (1.0 + jnp.exp(-gate_pre))
        silu = gate_pre * sig
        act_ref[e] = (silu * up_pre).astype(bf16)
        da = (grad_act * up_pre * sig * (1.0 + gate_pre * (1.0 - sig))).astype(bf16)
        db = (grad_act * silu).astype(bf16)
        da_ref[e] = da
        db_ref[e] = db
        backs.append((dot_nt(da, w_gate[e]) + dot_nt(db, w_up[e])).astype(bf16))
    for j in range(BLOCKS):
        at = slice(j * CAP, (j + 1) * CAP)
        back = dot_tn(picks[j], jnp.concatenate([backs[0][at], backs[1][at]], axis=0))
        target = near_ref if j < NEAR else across_ref
        target[j % NEAR] = back.astype(bf16)


def block_at(j, shape):
    def index(i, order):
        return (order[i * BLOCKS + j],) + (0,) * len(shape)

    return pl.BlockSpec((1,) + shape, index)


def expert_rows(width):
    return pl.BlockSpec((2, STEP, width), lambda i, *_: (0, i, 0))


def pair_block():
    return pl.BlockSpec((NEAR, TOK, D), lambda i, *_: (i, 0, 0))


def experts(order, rows, grads, gates, w_gate, w_up, w_down):
    slots = 16 * CAP
    return run(
        experts_body,
        [struct((8, TOK, D), bf16)] * 2
        + [struct((2, slots, D), bf16)] * 2
        + [struct((2, slots, 512), bf16)] * 3,
        [block_at(j, (TOK, D)) for j in range(BLOCKS)]
        + [block_at(j, (TOK, D)) for j in range(BLOCKS)]
        + [block_at(j, (2, TOK)) for j in range(BLOCKS)]
        + [once(w.shape) for w in (w_gate, w_up, w_down)],
        [pair_block(), pair_block(), expert_rows(D), expert_rows(D)] + [expert_rows(512)] * 3,
        (16 // BLOCKS,),
        (rows,) * BLOCKS + (grads,) * BLOCKS + (gates,) * BLOCKS + (w_gate, w_up, w_down),
        prefetch=order,
        micros=30,
    )


def expert_out_body(order, *refs):
    gates = refs[:BLOCKS]
    act, w_down, near_ref, across_ref = refs[BLOCKS:]
    outs = [dot(act[e], w_down[e]) for e in range(2)]
    for j in range(BLOCKS):
        pick, weight = choices(gates[j][0])
        at = slice(j * CAP, (j + 1) * CAP)
        both = jnp.concatenate([outs[0][at], outs[1][at]], axis=0) * weight
        target = near_ref if j < NEAR else across_ref
        target[j % NEAR] = dot_tn(pick, both.astype(bf16)).astype(bf16)


def expert_out(order, gates, act, w_down):
    slots = 16 * CAP
    return run(
        expert_out_body,
        [struct((8, TOK, D), bf16)] * 2,
        [block_at(j, (2, TOK)) for j in range(BLOCKS)] + [expert_rows(512), once(w_down.shape)],
        [pair_block(), pair_block()],
        (16 // BLOCKS,),
        (gates,) * BLOCKS + (act, w_down),
        prefetch=order,
        micros=13,
    )


def expert_grad_body(order, taken, graded, act, da, db, gate_ref, up_ref, down_ref):
    e = pl.program_id(0)
    gate_ref[0] = dot_tn(taken[0], da[0]).astype(bf16)
    up = dot_tn(taken[0], db[0]).astype(bf16)
    down_ref[0] = dot_tn(act[0], graded[0]).astype(bf16)
    for k in range(8):
        up_ref[order[k], e] = up[k * 192 : (k + 1) * 192]


def expert_grad(order, taken, graded, act, da, db):
    slots = 16 * CAP

    def one(rows, width):
        return pl.BlockSpec((1, rows, width), lambda e, *_: (e, 0, 0))

    return run(
        expert_grad_body,
        [struct((2, D, 512), bf16), struct((8, 2, 192, 512), bf16), struct((2, 512, D), bf16)],
        [one(slots, D), one(slots, D), one(slots, 512), one(slots, 512), one(slots, 512)],
        [one(D, 512), whole((8, 2, 192, 512)), one(512, D)],
        (2,),
        (taken, graded, act, da, db),
        prefetch=order,
        micros=14,
    )


def rms_scale(values):
    return lax.rsqrt(jnp.mean(values * values, axis=-1, keepdims=True) + norm_eps)


def three_parts(values):
    high = lax.reduce_precision(values, 8, 7)
    rest = values - high
    middle = lax.reduce_precision(rest, 8, 7)
    return [v.astype(bf16) for v in (high, middle, rest - middle)]


def shards(
    tokens,
    cotangent,
    segments,
    routes,
    gate_weights,
    w_query,
    w_key,
    w_value,
    w_out,
    norm_one,
    norm_two,
    w_gate,
    w_up,
    w_down,
):
    inputs = tokens[0].astype(f32)
    upstream = cotangent[0].astype(f32)
    yh, x = lax.axis_index("yh"), lax.axis_index("x")
    where = jnp.stack([x, yh]).astype(jnp.int32)
    order = jnp.stack(
        [
            (ahead("yl", m % 2) * 4 + ahead("z", m // 2)) * 2 + ahead("c", j // NEAR)
            for i in range(16 // BLOCKS)
            for j in range(BLOCKS)
            for m in (NEAR * i + j % NEAR,)
        ]
    ).astype(jnp.int32)
    batch_place = jnp.stack(
        [
            distance("c", b % 2) * 8 + distance("z", b // 2 % 4) * 2 + distance("yl", b // 8)
            for b in range(16)
        ]
    ).astype(jnp.int32)
    seq_place = jnp.stack(
        [distance("x", s % 4) * 2 + distance("yh", s // 4) for s in range(8)]
    ).astype(jnp.int32)

    def for_heads(weight, width):
        by_head = jnp.swapaxes(weight.reshape(-1, 8, width), 0, 1)
        return [by_head, jnp.concatenate([by_head[4:], by_head[:4]], axis=0)]

    gains = jnp.pad(jnp.stack([norm_one, norm_two], axis=1), ((0, 0), (0, 126)))
    strip = jnp.concatenate(
        for_heads(w_query, Q_OWN)
        + for_heads(w_key, HEAD_DIM)
        + for_heads(w_value, HEAD_DIM)
        + [jnp.broadcast_to(gains[None], (8,) + gains.shape)],
        axis=2,
    )
    strip = lax.all_to_all(strip, SEQ, 0, 0, tiled=True).reshape(96, 768)
    expert_ids = jnp.arange(EXPERTS, dtype=jnp.int32)[:, None, None]
    gate_dense = jnp.sum(jnp.where(routes[0][None] == expert_ids, gate_weights[0][None], 0.0), axis=2)
    strip = jnp.concatenate(
        [
            strip,
            jnp.concatenate(three_parts(gate_dense), axis=0),
            w_out.reshape(96, 192),
            shift(w_out, "yh", 1).reshape(96, 192),
        ],
        axis=1,
    )
    gathered = lax.all_gather(strip, BATCH, axis=0, tiled=True)
    grad_all = lax.all_gather(cotangent[0], BATCH, axis=0)

    feature = jnp.arange(D, dtype=jnp.int32)
    moved = feature % 192 // 12 * 96 + feature // 192 * 12 + feature % 12
    moving = (moved[:, None] == feature[None, :]).astype(bf16)
    pieces = ring_pieces(tokens[0], "x")
    xp, scale_half = prepare(where, pieces, moving)

    pack = jnp.concatenate([w_gate, w_up], axis=1)
    half_pack = pack.shape[1] // 2
    pack, _ = tie(pack, strip)
    pack_other = shift(pack, "yh", 1)
    pack, w_down, _, _ = tie(pack, w_down, pieces[2], pieces[3])
    down_below = shift(w_down, "x", 1)
    down_above = shift(w_down, "x", -1)
    pack_below = shift(pack, "x", 1)
    pack_above = shift(pack, "x", -1)

    def natural(row):
        return jnp.swapaxes(row.reshape(16, 8, 12), 0, 1).reshape(D)

    place = jnp.arange(2 * HALF, dtype=jnp.int32) + HALF * yh
    place = jnp.where(place >= 2 * HALF, place - 2 * HALF, place)
    seg = jnp.roll(segments[0], -HALF * yh)
    earlier = jnp.sum((seg[None, :] < seg[:, None]).astype(jnp.int32), axis=1)
    freq_index = jnp.arange(HEAD_DIM // 2, dtype=f32) * (2.0 / HEAD_DIM)
    frequency = jnp.tile(rope_base ** (-freq_index), 4)
    angle = (place - earlier).astype(f32)[:, None] * frequency
    cosine, sine = jnp.cos(angle), jnp.sin(angle)
    seg_row = seg[None, :]
    seg_col = jnp.broadcast_to(seg[:HALF, None], (HALF, 128))

    gathered, xp, pack_other, pack_below, pack_above, down_below, down_above = tie(
        gathered, xp, pack_other, pack_below, pack_above, down_below, down_above
    )
    down_low = shift(down_below[:1], "x", 1)
    down_high = shift(down_above[1:], "x", -1)
    pack_low = shift(pack_below[:, :half_pack], "x", 1)
    pack_high = shift(pack_above[:, half_pack:], "x", -1)

    normed, queries, own, sent = project(xp, scale_half, gathered, cosine, sine)
    other = shift(sent, "yh", 1)
    out_rows = gathered[:, 896:1088].reshape(192, D)
    out_other = gathered[:, 1088:].reshape(192, D)
    gain_one = natural(gathered[:, 640].astype(f32))
    gain_two = natural(gathered[:, 641].astype(f32))
    gates = jnp.sum(gathered[:, 768:896].reshape(16, 3, EXPERTS, TOK).astype(f32), axis=1)
    gates = lax.dynamic_slice_in_dim(gates, lax.axis_index(BATCH) * 2, 2, axis=1)
    mixed, partial = attend(where, queries, own, other, seg_col, seg_row, out_rows, out_other)
    partial, pack_low, pack_high, down_low, down_high = tie(
        partial, pack_low, pack_high, down_low, down_high
    )
    downs = [w_down, down_above, jnp.concatenate([down_low, down_high], axis=0), down_below]
    downs = jnp.stack(downs)
    downs_other = shift(downs, "yh", 1)
    hidden = inputs + reduce_ring(partial, "x")
    hidden, downs_other = tie(hidden, downs_other)
    pack_other, _ = tie(pack_other, hidden)
    other_below = shift(pack_other, "x", 1)
    other_above = shift(pack_other, "x", -1)
    downs = jnp.stack([downs, downs_other])
    downs = jnp.roll(jnp.roll(downs, yh, axis=0), x, axis=1)
    down_full = jnp.swapaxes(downs.reshape(8, 2, 64, D), 0, 1).reshape(2, 512, D)
    other_low = shift(other_below[:, :half_pack], "x", 1)
    other_high = shift(other_above[:, half_pack:], "x", -1)

    scale_two = rms_scale(hidden)
    normed_two = (hidden * scale_two * gain_two).astype(bf16)
    normed_all = lax.all_gather(normed_two, BATCH, axis=0)
    blocks = [
        pack,
        pack_above,
        jnp.concatenate([pack_low, pack_high], axis=1),
        pack_below,
        pack_other,
        other_above,
        jnp.concatenate([other_low, other_high], axis=1),
        other_below,
    ]
    gate_full = jnp.zeros((2, D, 512), bf16)
    up_full = jnp.zeros((2, D, 512), bf16)
    for k, block in enumerate(blocks):
        at = ahead("yh", k // 4) * 4 + ahead("x", k % 4)
        gate_full = lax.dynamic_update_slice(gate_full, block[:, :192], (0, at * 192, 0))
        up_full = lax.dynamic_update_slice(up_full, block[:, 192:384], (0, at * 192, 0))
    near, across, taken, graded, act, da, db = experts(
        order, normed_all, grad_all, gates, gate_full, up_full, down_full
    )
    got = shift(across, "c", 1)
    grad_gate, up_pack, grad_down = expert_grad(seq_place, taken, graded, act, da, db)
    up_pack, got = tie(up_pack, got)
    sum_gate = lax.psum_scatter(grad_gate, SEQ, scatter_dimension=1, tiled=True).astype(f32)
    sum_down = lax.psum_scatter(grad_down, SEQ, scatter_dimension=1, tiled=True).astype(f32)
    held = add_up(near, got).astype(bf16).reshape(4, 2, TOK, D)
    sent = ring_send(held, "z")
    act, _ = tie(act, held)
    out_near, out_across = expert_out(order, gates, act, down_full)
    out_near, out_across, *sent = tie(out_near, out_across, *sent)
    hops = ring_next(ring_add(held, sent), "z")
    up_pack = up_pack.reshape(4, 2, 2, 192, 512)
    up_sent = ring_send(up_pack, "x")
    total, *up_sent = tie(add_up(held[0], *hops), *up_sent)
    up_hops = ring_add(up_pack, up_sent)
    grad_normed_two = add_up(total[0], shift(total[1].astype(bf16), "yl", 1))

    scaled_two = gain_two * grad_normed_two
    grad_gain_two = jnp.sum(grad_normed_two * hidden * scale_two, axis=0)
    grad_hidden = (
        upstream
        + scale_two * scaled_two
        - hidden * scale_two**3 * jnp.mean(scaled_two * hidden, axis=-1, keepdims=True)
    )
    pieces = ring_pieces(grad_hidden.astype(bf16), "x")
    up_hops_0, up_hops_1, out_near, out_across, *pieces = tie(
        *up_hops, out_near, out_across, *pieces
    )
    out_got = shift(out_across, "c", 1)
    up_hops = ring_next((up_hops_0, up_hops_1), "x")
    back = attend_back(
        where, queries, mixed, own, other, seg_col, seg_row, out_rows, out_other, pieces, cosine, sine
    )
    *back, out_got, up_got_0, up_got_1 = tie(*back, out_got, *up_hops)
    grad_query, grad_own, grad_sent, grad_out_w = back
    up_total = add_up(up_pack[0], up_got_0, up_got_1)
    held = add_up(out_near, out_got).astype(bf16).reshape(4, 2, TOK, D)
    grad_out_w = jnp.swapaxes(grad_out_w.reshape(2, 16, 96, 192), 0, 1)
    grad_out_w = jnp.swapaxes(grad_out_w, 1, 2).reshape(16, 96, 384)
    grad_got = shift(grad_sent, "yh", 1)
    sent = ring_send(held, "z")
    grad_got, *sent = tie(grad_got, *sent)
    hops = ring_next(ring_add(held, sent), "z")
    back = unproject(where, grad_query, grad_own, grad_got, gathered, moving, xp, scale_half)
    *back, hop_0, hop_1 = tie(*back, *hops)
    grad_raw, grad_part, gain_one_part = back
    total = add_up(held[0], hop_0, hop_1)
    out_last = shift(total[1].astype(bf16), "yl", 1)
    up_last = shift(up_total[1].astype(bf16), "yh", 1)
    sent = ring_send(grad_part, "x")
    out_last, up_last, *sent = tie(out_last, up_last, *sent)
    output = hidden + add_up(total[0], out_last)
    sum_up = add_up(up_total[0], up_last)
    grad_normed_one = add_up(grad_part[0], *ring_next(ring_add(grad_part, sent), "x"))
    scaled_one = gain_one * grad_normed_one
    scale_one = rms_scale(inputs)
    grad_inputs = (
        grad_hidden
        + scale_one * scaled_one
        - inputs * scale_one**3 * jnp.mean(scaled_one * inputs, axis=-1, keepdims=True)
    )

    gain_two_part = jnp.swapaxes(grad_gain_two.reshape(8, 16, 12), 0, 1).reshape(1, D)
    gain_rows = jnp.concatenate([gain_one_part[:1], gain_two_part, jnp.zeros((6, D), f32)], axis=0)
    grad_w = weight_grad(batch_place, normed, grad_raw, gain_rows, grad_out_w)
    grad_w = reduce_batch(grad_w[:8], grad_w[8:])
    sum_out = add_up(grad_w[:, 768:960], shift(grad_w[:, 960:].astype(bf16), "yh", 1))
    sum_out = sum_out.reshape(12, D)
    grad_w = grad_w[:, :768].astype(bf16).reshape(8, 12, 768)
    grad_w = lax.all_to_all(grad_w, SEQ, 0, 0, tiled=True).astype(f32)

    def from_heads(first, width):
        total = grad_w[:, :, first : first + width]
        second = grad_w[:, :, first + width : first + 2 * width]
        total = total + jnp.concatenate([second[4:], second[:4]], axis=0)
        return jnp.swapaxes(total, 0, 1).reshape(12, 8 * width)

    gain_sum = jnp.sum(grad_w[:, :, 640:642], axis=0)
    return (
        output.astype(bf16)[None],
        grad_inputs.astype(bf16)[None],
        from_heads(0, Q_OWN),
        from_heads(2 * Q_OWN, HEAD_DIM),
        from_heads(2 * Q_OWN + 2 * HEAD_DIM, HEAD_DIM),
        sum_out,
        gain_sum[:, 0],
        gain_sum[:, 1],
        sum_gate,
        sum_up,
        sum_down,
    )


def solution(mesh):
    fine = Mesh(mesh.devices.reshape(2, 4, 2, 4, 2), SEQ + BATCH)
    both = SEQ + BATCH
    placed = (
        P(BATCH, SEQ, None),
        P(BATCH, SEQ, None),
        P(BATCH, None),
        P(BATCH, SEQ, None),
        P(BATCH, SEQ, None),
        P(both, None),
        P(both, None),
        P(both, None),
        P(both, None),
        P(both),
        P(both),
        P(BATCH, SEQ, None),
        P(BATCH, SEQ, None),
        P(BATCH, SEQ, None),
    )
    return jax.shard_map(
        shards,
        mesh=fine,
        in_specs=placed,
        out_specs=(
            P(BATCH, SEQ, None),
            P(BATCH, SEQ, None),
            P(both, None),
            P(both, None),
            P(both, None),
            P(both, None),
            P(both),
            P(both),
            P(BATCH, SEQ, None),
            P(BATCH, SEQ, None),
            P(BATCH, SEQ, None),
        ),
        check_vma=False,
    )
```

time: 808 us -> 508 us (0.63)
  waiting for transfers between devices: 321 us -> 142 us
  Pallas kernels: 0 us -> 123 us
  matrix products: 99.8 us -> 0 us
  other arithmetic: 117 us -> 51.8 us
  blocking collectives: 40.1 us -> 0 us
  starting transfers between devices: 135 us -> 95.4 us
    all_gather x4 -> x1, waiting for transfers between devices: 170 us -> 0.02 us  [shards(): gathered = lax.all_gather(strip, BATCH, axis=0, tiled=True)]
    pallas_call x0 -> x9, Pallas kernels: none -> 123 us  [run(): pl.pallas_call(body, grid_spec=spec, out_shape=out_shapes, compiler_param...]
    dot_general x25 -> x0, matrix products: 99.8 us -> none  [the longest x4 9.17 us: dot(): return jnp.dot(a, b, preferred_element_type=f32)]
    ppermute x87 -> x57, starting transfers between devices: 128 us -> 86.8 us  [shift(): lax.ppermute(value, axis, [(i, (i + by) % size) for i in range(size)])]
    all_gather x2 -> x0, blocking collectives: 40.1 us -> none  [the longest x1 20.6 us: shards(): gains = lax.all_gather(gains, BATCH, axis=0, tiled=True)]
    concatenate x53 -> x20, other arithmetic: 48.6 us -> 9.12 us  [the longest x2 5.18 us: shards(): downs = jnp.roll(jnp.roll(downs, yh, axis=0), x, axis=1)]
    unnamed x168 -> x73, local copies, waits for them, and re-layouts: 22.1 us -> 1.32 us
    dynamic_update_slice x0 -> x11, local copies, waits for them, and re-layouts: none -> 16.7 us  [the longest x7 11.6 us: shards(): lax.dynamic_update_slice(up_full, block[:, 192:384], (0, at * 192, 0))]
  transfers between devices with their start and end apart: 95 -> 64, of which waited for: 43 -> 27; matrix products, arithmetic and copies ran while one was open for 27% -> 23% of each run, Pallas kernels for 0% -> 19%
where the time goes in v2:
time: 508 us; the launch traced here: 499 us
  waiting for transfers between devices  142 us (28%)
  Pallas kernels  123 us (24%)
  starting transfers between devices  95.4 us (19%)
  local copies, waits for them, and re-layouts  70.8 us (14%)
  other arithmetic  51.8 us (10%)
  between operations  15.2 us (3%)
    ppermute x57, waiting for transfers between devices, shift(): lax.ppermute(value, axis, [(i, (i + by) % size) for i in range(size)])  127 us
    pallas_call x9, Pallas kernels, run(): pl.pallas_call(body, grid_spec=spec, out_shape=out_shapes, compiler_param...  123 us
    ppermute x57, starting transfers between devices, shift(): lax.ppermute(value, axis, [(i, (i + by) % size) for i in range(size)])  86.8 us
    dynamic_update_slice x7, local copies, waits for them, and re-layouts, shards(): lax.dynamic_update_slice(up_full, block[:, 192:384], (0, at * 192, 0))  11.6 us
  transfers between devices with their start and end apart: 64, of which 27 were waited for; matrix products, arithmetic and copies ran while one was open for 23% of the time, Pallas kernels for 19%

profile of v2, /device:TPU:8, one launch (start us, length us, event | category | flops | bytes accessed | tf_op | source)
XLA Modules:
  0.0 498.5 jit_solution(6503503502263108019)
XLA Ops:
  13.9 5.0 all-to-all-start
  20.7 6.6 %all-to-all-done = bf16[8,12,768]{2,1,0:T(8,128)(2,1)S(1)} async-done(((bf16[8,12,768]{2,1,0:T(8,128)(2,1)}), bf16[8,12,768]{2,1,0:T(8,128)(2,1)S(1)}, u32[]{:S(2)}, u32[]{:S(2)}) %all-to-all-start) | async-done | bytes 147488 | tf_op jit(solution)/shard_map/all_to_all | solution.py:653
  53.2 7.5 %shard_map.221 = (bf16[512,1536]{1,0:T(8,128)(2,1)}, f32[512,128]{1,0:T(8,128)}) custom-call(s32[2]{0:T(128)} %pad_add_fusion.where, bf16[128,1536]{1,0:T(8,128)(2,1)} %bitcast.170, bf16[128,1536]{1,0:T(8,128)(2,1)} %copy-done.24, bf16[64,1536]{1,0:T(8,128)(2,1)} %copy-done.34, bf16[64,1536]{1,0:T(8,128)(2,1)} %copy-done.35, bf16[128,1536]{1,0:T(8,128)(2,1)} %copy-done.23, ...), custom_call_target="tpu_custom_call" | custom-call | flops 7699999744 | tf_op jit(solution)/shard_map/pallas_call | solution.py:121
  66.0 10.3 %collective-permute-done.5 = bf16[2,384,512]{2,1,0:T(8,128)(2,1)} collective-permute-done((bf16[2,384,512]{2,1,0:T(8,128)(2,1)S(1)}, bf16[2,384,512]{2,1,0:T(8,128)(2,1)}, u32[]{:S(2)}, u32[]{:S(2)}) %collective-permute-start.5) | collective-permute-done | bytes 786464 | tf_op jit(solution)/shard_map/ppermute | solution.py:32
  80.6 5.1 %shard_map.222 = (bf16[512,1536]{1,0:T(8,128)(2,1)}, bf16[512,384]{1,0:T(8,128)(2,1)}, bf16[512,256]{1,0:T(8,128)(2,1)}, bf16[512,256]{1,0:T(8,128)(2,1)}) custom-call(bf16[512,1536]{1,0:T(8,128)(2,1)} %get-tuple-element.97.xp, f32[512,128]{1,0:T(8,128)} %get-tuple-element.98.scale, bf16[1536,1280]{1,0:T(8,128)(2,1)} %all-gather.5.cloned.1.call-done.weight, ...), custom_call_target="tpu_custom_call" | custom-call | flops 5500000256 | tf_op jit(solution)/shard_map/pallas_call | solution.py:121
  94.2 6.9 %collective-permute-done.10.other = bf16[512,256]{1,0:T(8,128)(2,1)} collective-permute-done((bf16[512,256]{1,0:T(8,128)(2,1)}, bf16[512,256]{1,0:T(8,128)(2,1)}, u32[]{:S(2)}, u32[]{:S(2)}) %collective-permute-start.10) | collective-permute-done | bytes 262176 | tf_op jit(solution)/shard_map/ppermute | solution.py:32
  102.0 14.8 %shard_map.223 = (bf16[512,384]{1,0:T(8,128)(2,1)}, bf16[4,128,1536]{2,1,0:T(8,128)(2,1)}) custom-call(s32[2]{0:T(128)} %pad_add_fusion.where, bf16[512,384]{1,0:T(8,128)(2,1)} %get-tuple-element.100.q, bf16[512,256]{1,0:T(8,128)(2,1)} %get-tuple-element.101.own, bf16[512,256]{1,0:T(8,128)(2,1)} %collective-permute-done.10.other, ...), custom_call_target="tpu_custom_call" | custom-call | flops 16499999744 | tf_op jit(solution)/shard_map/pallas_call | solution.py:121
  141.5 18.2 %collective-permute-done.19 = bf16[4,2,64,1536]{3,2,1,0:T(8,128)(2,1)} collective-permute-done((bf16[4,2,64,1536]{3,2,1,0:T(8,128)(2,1)}, bf16[4,2,64,1536]{3,2,1,0:T(8,128)(2,1)}, u32[]{:S(2)}, u32[]{:S(2)}) %collective-permute-start.19) | collective-permute-done | bytes 1572896 | tf_op jit(solution)/shard_map/ppermute | solution.py:32
  171.1 6.0 %collective-permute-done.20 = bf16[2,384,512]{2,1,0:T(8,128)(2,1)} collective-permute-done((bf16[2,384,512]{2,1,0:T(8,128)(2,1)}, bf16[2,384,512]{2,1,0:T(8,128)(2,1)}, u32[]{:S(2)}, u32[]{:S(2)}) %collective-permute-start.20) | collective-permute-done | bytes 786464 | tf_op jit(solution)/shard_map/ppermute | solution.py:32
  203.2 30.3 %shard_map.224 = (bf16[8,128,1536]{2,1,0:T(8,128)(2,1)}, bf16[8,128,1536]{2,1,0:T(8,128)(2,1)}, bf16[2,768,1536]{2,1,0:T(8,128)(2,1)}, bf16[2,768,1536]{2,1,0:T(...) custom-call(s32[16]{0:T(128)} %stack.205.order, ...), custom_call_target="tpu_custom_call" | custom-call | flops 32999999488 | tf_op jit(solution)/shard_map/pallas_call | solution.py:121
  234.8 12.9 %shard_map.225 = (bf16[2,1536,512]{2,1,0:T(8,128)(2,1)}, bf16[8,2,192,512]{3,2,1,0:T(8,128)(2,1)}, bf16[2,512,1536]{2,1,0:T(8,128)(2,1)}) custom-call(s32[8]{0:T(128)} %stack.188.order, bf16[2,768,1536]{2,1,0:T(8,128)(2,1)} %get-tuple-element.117.taken, bf16[2,768,1536]{2,1,0:T(8,128)(2,1)} %get-tuple-element.118.graded, ...), custom_call_target="tpu_custom_call" | custom-call | flops 15399999488 | tf_op jit(solution)/shard_map/pallas_call | solution.py:121
  254.0 13.6 %shard_map.226 = (bf16[8,128,1536]{2,1,0:T(8,128)(2,1)}, bf16[8,128,1536]{2,1,0:T(8,128)(2,1)}) custom-call(s32[16]{0:T(128)} %stack.205.order, f32[16,2,128]{2,1,0:T(2,128)} %constant_dynamic-slice_fusion.refs_16_.refs_17_.refs_18_.refs_19_.refs_20_.refs_21_.refs_22_.refs_23_.refs_0_.refs_1_.refs_2_.refs_3_.refs_4_.refs_5_.refs_6_.refs_7_, ...), custom_call_target="tpu_custom_call" | custom-call | flops 14300000256 | tf_op jit(solution)/shard_map/pallas_call | solution.py:121
  274.2 13.6 %collective-permute-done.28 = bf16[2,128,1536]{2,1,0:T(8,128)(2,1)S(1)} collective-permute-done((bf16[2,128,1536]{2,1,0:T(8,128)(2,1)S(1)}, bf16[2,128,1536]{2,1,0:T(8,128)(2,1)S(1)}, u32[]{:S(2)}, u32[]{:S(2)}) %collective-permute-start.28) | collective-permute-done | bytes 786464 | tf_op jit(solution)/shard_map/ppermute | solution.py:32
  293.6 12.3 %collective-permute-done.31 = bf16[128,1536]{1,0:T(8,128)(2,1)S(1)} collective-permute-done((bf16[128,1536]{1,0:T(8,128)(2,1)S(1)}, bf16[128,1536]{1,0:T(8,128)(2,1)S(1)}, u32[]{:S(2)}, u32[]{:S(2)}) %collective-permute-start.31) | collective-permute-done | bytes 393248 | tf_op jit(solution)/shard_map/ppermute | solution.py:32
  310.8 6.7 %collective-permute-done.33.z3 = bf16[128,1536]{1,0:T(8,128)(2,1)S(1)} collective-permute-done((bf16[128,1536]{1,0:T(8,128)(2,1)S(1)}, bf16[128,1536]{1,0:T(8,128)(2,1)S(1)}, u32[]{:S(2)}, u32[]{:S(2)}) %collective-permute-start.33) | collective-permute-done | bytes 393248 | tf_op jit(solution)/shard_map/ppermute | solution.py:32
  335.5 22.3 %shard_map.227 = (bf16[512,384]{1,0:T(8,128)(2,1)}, f32[512,256]{1,0:T(8,128)}, bf16[512,256]{1,0:T(8,128)(2,1)}, bf16[384,1536]{1,0:T(8,128)(2,1)}) custom-call(s32[2]{0:T(128)} %pad_add_fusion.where, bf16[512,384]{1,0:T(8,128)(2,1)} %get-tuple-element.100.q, bf16[512,384]{1,0:T(8,128)(2,1)} %get-tuple-element.137.att, ...), custom_call_target="tpu_custom_call" | custom-call | flops 24199999488 | tf_op jit(solution)/shard_map/pallas_call | solution.py:121
  387.0 9.9 %shard_map.228 = (bf16[512,640]{1,0:T(8,128)(2,1)}, bf16[4,128,1536]{2,1,0:T(8,128)(2,1)}, f32[8,1536]{1,0:T(8,128)}) custom-call(s32[2]{0:T(128)} %pad_add_fusion.where, bf16[512,384]{1,0:T(8,128)(2,1)} %get-tuple-element.151.q, f32[512,256]{1,0:T(8,128)} %get-tuple-element.152.own, bf16[512,256]{1,0:T(8,128)(2,1)} %collective-permute-done.39.got, ...), custom_call_target="tpu_custom_call" | custom-call | flops 11000000512 | tf_op jit(solution)/shard_map/pallas_call | solution.py:121
  397.0 5.3 %collective-permute-done.42 = bf16[2,128,1536]{2,1,0:T(8,128)(2,1)S(1)} collective-permute-done((bf16[2,128,1536]{2,1,0:T(8,128)(2,1)S(1)}, bf16[2,128,1536]{2,1,0:T(8,128)(2,1)S(1)}, u32[]{:S(2)}, u32[]{:S(2)}) %collective-permute-start.42) | collective-permute-done | bytes 786464 | tf_op jit(solution)/shard_map/ppermute | solution.py:32
  405.3 4.8 collective-permute-start.44
  410.8 6.7 %shard_map.229 = bf16[16,96,1152]{2,1,0:T(8,128)(2,1)} custom-call(s32[16]{0:T(128)} %stack.224.order, bf16[512,1536]{1,0:T(8,128)(2,1)} %get-tuple-element.168.normed, bf16[512,640]{1,0:T(8,128)(2,1)} %get-tuple-element.169.raw, f32[8,1536]{1,0:T(8,128)} %maximum_maximum_fusion.gains, bf16[16,96,384]{2,1,0:T(8,128)(2,1)} %reshape.285.out_rows), custom_call_target="tpu_custom_call" | custom-call | flops 6600000000 | tf_op jit(solution)/shard_map/pallas_call | solution.py:121
  445.6 4.9 collective-permute-done.51
  457.5 4.6 collective-permute-done.54
  466.0 5.9 %collective-permute-done.55 = bf16[96,1152]{1,0:T(8,128)(2,1)S(1)} collective-permute-done((bf16[96,1152]{1,0:T(8,128)(2,1)S(1)}, bf16[96,1152]{1,0:T(8,128)(2,1)S(1)}, u32[]{:S(2)}, u32[]{:S(2)}) %collective-permute-start.55) | collective-permute-done | bytes 221216 | tf_op jit(solution)/shard_map/ppermute | solution.py:32
  480.7 7.6 %all-to-all-done.1 = bf16[8,12,768]{2,1,0:T(8,128)(2,1)S(1)} async-done(((bf16[8,12,768]{2,1,0:T(8,128)(2,1)}), bf16[8,12,768]{2,1,0:T(8,128)(2,1)S(1)}, u32[]{:S(2)}, u32[]{:S(2)}) %all-to-all-start.1) | async-done | bytes 147488 | tf_op jit(solution)/shard_map/all_to_all | solution.py:823
  (349 shorter events, 241.4 us)
Async XLA Ops:
  18.9 57.5 %all-gather.5.cloned.1.call-start = ((), (), s32[]{:S(2)}) async-start(), calls=%async_computation.4 | async-start | bytes 4177920 | tf_op jit(solution)/shard_map/all_gather | solution.py:665
  28.2 174.8 %all-gather.7.cloned.1.call-start = ((), (), s32[]{:S(2)}) async-start(), calls=%async_computation.5 | async-start | bytes 6684672 | tf_op jit(solution)/shard_map/all_gather | solution.py:666
  28.9 174.3 %all-gather.9.cloned.1.call-start = ((), (), s32[]{:S(2)}) async-start(), calls=%async_computation.8 | async-start | bytes 6684672 | tf_op jit(solution)/shard_map/all_gather | solution.py:734
  46.1 30.1 %collective-permute-start.5 = (bf16[2,384,512]{2,1,0:T(8,128)(2,1)S(1)}, bf16[2,384,512]{2,1,0:T(8,128)(2,1)}, u32[]{:S(2)}, u32[]{:S(2)}) collective-permute-start(bf16[2,384,512]{2,1,0:T(8,128)(2,1)S(1)} %pad_maximum_fusion.1), channel_id=1, source_target_pairs={{0,64},{64,0},{1,65},{65,1},{2,66},{66,2},{3,67},{67,3},{4,68},{68... | collective-permute-start | bytes 2359304 | tf_op jit(solution)/shard_map/ppermute | solution.py:32
  46.7 29.6 %collective-permute-start.9 = (bf16[2,64,1536]{2,1,0:T(8,128)(2,1)}, bf16[2,64,1536]{2,1,0:T(8,128)(2,1)S(1)}, u32[]{:S(2)}, u32[]{:S(2)}) collective-permute-start(bf16[2,64,1536]{2,1,0:T(8,128)(2,1)} %param.27), channel_id=1, source_target_pairs={{0,48},{16,0},{32,16},{48,32},{1,49},{17,1},{33,17},{49,33},{2,50}... | collective-permute-start | bytes 1179656 | tf_op jit(solution)/shard_map/ppermute | solution.py:32
  50.0 26.3 %collective-permute-start.8 = (bf16[2,64,1536]{2,1,0:T(8,128)(2,1)}, bf16[2,64,1536]{2,1,0:T(8,128)(2,1)S(1)}, u32[]{:S(2)}, u32[]{:S(2)}) collective-permute-start(bf16[2,64,1536]{2,1,0:T(8,128)(2,1)} %param.27), channel_id=1, source_target_pairs={{0,16},{16,32},{32,48},{48,0},{1,17},{17,33},{33,49},{49,1},{2,18}... | collective-permute-start | bytes 1179656 | tf_op jit(solution)/shard_map/ppermute | solution.py:32
  50.0 26.3 %collective-permute-start.7 = (bf16[2,384,512]{2,1,0:T(8,128)(2,1)S(1)}, bf16[2,384,512]{2,1,0:T(8,128)(2,1)S(1)}, u32[]{:S(2)}, u32[]{:S(2)}) collective-permute-start(bf16[2,384,512]{2,1,0:T(8,128)(2,1)S(1)} %pad_maximum_fusion.1), channel_id=1, source_target_pairs={{0,48},{16,0},{32,16},{48,32},{1,49},{17,1},{33,17},{49,33},{2,50}... | collective-permute-start | bytes 2359304 | tf_op jit(solution)/shard_map/ppermute | solution.py:32
  53.2 23.1 %collective-permute-start.6 = (bf16[2,384,512]{2,1,0:T(8,128)(2,1)S(1)}, bf16[2,384,512]{2,1,0:T(8,128)(2,1)S(1)}, u32[]{:S(2)}, u32[]{:S(2)}) collective-permute-start(bf16[2,384,512]{2,1,0:T(8,128)(2,1)S(1)} %pad_maximum_fusion.1), channel_id=1, source_target_pairs={{0,16},{16,32},{32,48},{48,0},{1,17},{17,33},{33,49},{49,1},{2,18}... | collective-permute-start | bytes 2359304 | tf_op jit(solution)/shard_map/ppermute | solution.py:32
  77.8 38.9 %collective-permute-start.14 = (bf16[1,64,1536]{2,1,0:T(8,128)(2,1)}, bf16[1,64,1536]{2,1,0:T(8,128)(2,1)}, u32[]{:S(2)}, u32[]{:S(2)}) collective-permute-start(bf16[1,64,1536]{2,1,0:T(8,128)(2,1)} %slice.455), channel_id=1, source_target_pairs={{0,48},{16,0},{32,16},{48,32},{1,49},{17,1},{33,17},{49,33},{2,50}... | collective-permute-start | bytes 589832 | tf_op jit(solution)/shard_map/ppermute | solution.py:32
  79.5 37.3 %collective-permute-start.13 = (bf16[1,64,1536]{2,1,0:T(8,128)(2,1)}, bf16[1,64,1536]{2,1,0:T(8,128)(2,1)}, u32[]{:S(2)}, u32[]{:S(2)}) collective-permute-start(bf16[1,64,1536]{2,1,0:T(8,128)(2,1)} %slice.454), channel_id=1, source_target_pairs={{0,16},{16,32},{32,48},{48,0},{1,17},{17,33},{33,49},{49,1},{2,18}... | collective-permute-start | bytes 589832 | tf_op jit(solution)/shard_map/ppermute | solution.py:32
  79.9 36.9 %collective-permute-start.11 = (bf16[2,192,512]{2,1,0:T(8,128)(2,1)S(1)}, bf16[2,192,512]{2,1,0:T(8,128)(2,1)}, u32[]{:S(2)}, u32[]{:S(2)}) collective-permute-start(bf16[2,192,512]{2,1,0:T(8,128)(2,1)S(1)} %slice.452), channel_id=1, source_target_pairs={{0,16},{16,32},{32,48},{48,0},{1,17},{17,33},{33,49},{49,1},{2,18}... | collective-permute-start | bytes 1179656 | tf_op jit(solution)/shard_map/ppermute | solution.py:32
  88.7 28.1 %collective-permute-start.12 = (bf16[2,192,512]{2,1,0:T(8,128)(2,1)}, bf16[2,192,512]{2,1,0:T(8,128)(2,1)S(1)}, u32[]{:S(2)}, u32[]{:S(2)}) collective-permute-start(bf16[2,192,512]{2,1,0:T(8,128)(2,1)} %get-tuple-element.237), channel_id=1, source_target_pairs={{0,48},{16,0},{32,16},{48,32},{1,49},{17,1},{33,17},{49,33},{2,50}... | collective-permute-start | bytes 1179656 | tf_op jit(solution)/shard_map/ppermute | solution.py:32
  125.1 34.5 %collective-permute-start.19 = (bf16[4,2,64,1536]{3,2,1,0:T(8,128)(2,1)}, bf16[4,2,64,1536]{3,2,1,0:T(8,128)(2,1)}, u32[]{:S(2)}, u32[]{:S(2)}) collective-permute-start(bf16[4,2,64,1536]{3,2,1,0:T(8,128)(2,1)} %get-tuple-element.220), channel_id=1, source_target_pairs={{0,64},{64,0},{1,65},{65,1},{2,66},{66,2},{3,67},{67,3},{4,68},{68... | collective-permute-start | bytes 4718600 | tf_op jit(solution)/shard_map/ppermute | solution.py:32
  161.3 267.0 %reduce-scatter.5.cloned.1.call-start = ((), (), s32[]{:S(2)}) async-start(), calls=%async_computation.7 | async-start | bytes 3538944 | tf_op jit(solution)/shard_map/reduce_scatter | solution.py:758
  168.7 20.3 %collective-permute-start.21 = (bf16[2,384,512]{2,1,0:T(8,128)(2,1)}, bf16[2,384,512]{2,1,0:T(8,128)(2,1)}, u32[]{:S(2)}, u32[]{:S(2)}) collective-permute-start(bf16[2,384,512]{2,1,0:T(8,128)(2,1)} %collective-permute-done.5), channel_id=1, source_target_pairs={{0,16},{16,32},{32,48},{48,0},{1,17},{17,33},{33,49},{49,1},{2,18}... | collective-permute-start | bytes 2359304 | tf_op jit(solution)/shard_map/ppermute | solution.py:32
  247.7 182.5 %reduce-scatter.3.cloned.1.call-start = ((), (), s32[]{:S(2)}) async-start(), calls=%async_computation.6 | async-start | bytes 3538944 | tf_op jit(solution)/shard_map/reduce_scatter | solution.py:757
  271.3 20.2 %collective-permute-start.27 = (bf16[2,128,1536]{2,1,0:T(8,128)(2,1)S(1)}, bf16[2,128,1536]{2,1,0:T(8,128)(2,1)S(1)}, u32[]{:S(2)}, u32[]{:S(2)}) collective-permute-start(bf16[2,128,1536]{2,1,0:T(8,128)(2,1)S(1)} %pad_maximum_fusion.2), channel_id=1, source_target_pairs={{0,2},{2,4},{4,6},{6,0},{1,3},{3,5},{5,7},{7,1},{8,10},{10,12},{12... | collective-permute-start | bytes 2359304 | tf_op jit(solution)/shard_map/ppermute | solution.py:32
  271.5 20.2 %collective-permute-start.30 = (bf16[1,2,192,512]{3,2,1,0:T(8,128)(2,1)S(1)}, bf16[1,2,192,512]{3,2,1,0:T(8,128)(2,1)S(1)}, u32[]{:S(2)}, u32[]{:S(2)}) collective-permute-start(bf16[1,2,192,512]{3,2,1,0:T(8,128)(2,1)S(1)} %get-tuple-element.197), channel_id=1, source_target_pairs={{0,48},{16,0},{32,16},{48,32},{1,49},{17,1},{33,17},{49,33},{2,50}... | collective-permute-start | bytes 1179656 | tf_op jit(solution)/shard_map/ppermute | solution.py:32
  327.2 31.1 %collective-permute-start.36 = (bf16[8,128,1536]{2,1,0:T(8,128)(2,1)}, bf16[8,128,1536]{2,1,0:T(8,128)(2,1)}, u32[]{:S(2)}, u32[]{:S(2)}) collective-permute-start(bf16[8,128,1536]{2,1,0:T(8,128)(2,1)} %get-tuple-element.147), channel_id=1, source_target_pairs={{0,1},{1,0},{2,3},{3,2},{4,5},{5,4},{6,7},{7,6},{8,9},{9,8},{10,11... | collective-permute-start | bytes 9437192 | tf_op jit(solution)/shard_map/ppermute | solution.py:32
  331.6 26.1 %collective-permute-start.37 = (bf16[2,2,192,512]{3,2,1,0:T(8,128)(2,1)S(1)}, bf16[2,2,192,512]{3,2,1,0:T(8,128)(2,1)S(1)}, u32[]{:S(2)}, u32[]{:S(2)}) collective-permute-start(bf16[2,2,192,512]{3,2,1,0:T(8,128)(2,1)S(1)} %pad_maximum_fusion.4), channel_id=1, source_target_pairs={{0,16},{16,32},{32,48},{48,0},{1,17},{17,33},{33,49},{49,1},{2,18}... | collective-permute-start | bytes 2359304 | tf_op jit(solution)/shard_map/ppermute | solution.py:32
  333.7 24.6 %collective-permute-start.38 = (bf16[2,2,192,512]{3,2,1,0:T(8,128)(2,1)S(1)}, bf16[2,2,192,512]{3,2,1,0:T(8,128)(2,1)S(1)}, u32[]{:S(2)}, u32[]{:S(2)}) collective-permute-start(bf16[2,2,192,512]{3,2,1,0:T(8,128)(2,1)S(1)} %pad_maximum_fusion.5), channel_id=1, source_target_pairs={{0,48},{16,0},{32,16},{48,32},{1,49},{17,1},{33,17},{49,33},{2,50}... | collective-permute-start | bytes 2359304 | tf_op jit(solution)/shard_map/ppermute | solution.py:32
  358.2 23.7 %collective-permute-start.39 = (bf16[512,256]{1,0:T(8,128)(2,1)}, bf16[512,256]{1,0:T(8,128)(2,1)}, u32[]{:S(2)}, u32[]{:S(2)}) collective-permute-start(bf16[512,256]{1,0:T(8,128)(2,1)} %get-tuple-element.153), channel_id=1, source_target_pairs={{0,64},{64,0},{1,65},{65,1},{2,66},{66,2},{3,67},{67,3},{4,68},{68... | collective-permute-start | bytes 786440 | tf_op jit(solution)/shard_map/ppermute | solution.py:32
  371.5 60.8 %collective-permute-start.45 = (bf16[2,192,512]{2,1,0:T(8,128)(2,1)}, bf16[2,192,512]{2,1,0:T(8,128)(2,1)}, u32[]{:S(2)}, u32[]{:S(2)}) collective-permute-start(bf16[2,192,512]{2,1,0:T(8,128)(2,1)} %fusion.22), channel_id=1, source_target_pairs={{0,64},{64,0},{1,65},{65,1},{2,66},{66,2},{3,67},{67,3},{4,68},{68... | collective-permute-start | bytes 1179656 | tf_op jit(solution)/shard_map/ppermute | solution.py:32
  405.3 28.3 %collective-permute-start.44 = (bf16[128,1536]{1,0:T(8,128)(2,1)}, bf16[128,1536]{1,0:T(8,128)(2,1)}, u32[]{:S(2)}, u32[]{:S(2)}) collective-permute-start(bf16[128,1536]{1,0:T(8,128)(2,1)} %fusion.21), channel_id=1, source_target_pairs={{0,8},{8,0},{1,9},{9,1},{2,10},{10,2},{3,11},{11,3},{4,12},{12,4},... | collective-permute-start | bytes 1179656 | tf_op jit(solution)/shard_map/ppermute | solution.py:32
  (77 other events, 924.2 us)
Sparse Core Ops, SparseCore 0:
  28.3 42.9 all-gather.4
  73.0 48.7 all-gather.6
  161.4 41.8 all-gather.8
  247.8 84.9 reduce-scatter.4
  337.1 88.9 reduce-scatter.2
